TPU v7x, 512 devices: a whole 4x4x16 slice. The times are simulated.
512 devices in a mesh: member: 32 (over y_hi, z), lat: 8 (over y_lo, x), lev: 2 (over core).
Axes of the slice: x: 4, y: 4 (y_hi: 2, y_lo: 2; y = y_hi * 2 + y_lo), z: 16, core: 2. Of those that a mesh axis runs over, the one named last changes fastest.
Arguments:
- alpha_field: float32 [32, 8, 640, 1280], P('member', 'lev', 'lat'), may hold values from -1.0606601 to 1.0606601
- perturbation: bfloat16 [32, 8, 640, 1280], P('member', 'lev', 'lat'), may hold values from -6 to 6
- obs_value: float32 [8, 640, 1280], P('lev', 'lat', 'member'), may hold values from -6 to 6
- obs_mask: int32 [8, 640, 1280], P('lev', 'lat', 'member'), may hold values 0 or 1
- obs_precision: float32 [8], P('lev'), may hold values from 0.5 to 2
- loc_width: int32 [8], P('lev'), may hold values from 6 to 24, as said below
Outputs:
- gradient: float32 [32, 8, 640, 1280], P('member', 'lev', 'lat')
- increment: float32 [8, 640, 1280], P('lev', 'lat', 'member')
Inputs may be any that keep to these rules, and one draw needn't show every extreme that they name: `loc_width`: one length scale a level; some level has the smallest and some the largest value.
All inputs are finite; a program needn't handle non-finite values. No bound on the sum of `obs_mask` on one device may be relied on, other than what follows from the above.
Results may differ from a plain program's by a relative error of at most 0.0059.
Values may be sent and summed in bfloat16 or wider, within the bound.
A program may use at most 64 MiB of HBM per device.

v0:
```python
import jax
import jax.numpy as jnp
from jax import lax
from jax.sharding import PartitionSpec as P

HALO = 24


vert_scale = 2.0


def extended(cells, sides, width):
    for axis, dim in sides:
        count = lax.axis_size(axis)
        ends = count - 1
        head = lax.slice_in_dim(cells, 0, width, axis=dim)
        tail = lax.slice_in_dim(cells, cells.shape[dim] - width, cells.shape[dim], axis=dim)
        cells = jnp.concatenate(
            [
                lax.ppermute(tail, axis, [(i, (i + 1) % count) for i in range(ends)]),
                cells,
                lax.ppermute(head, axis, [((i + 1) % count, i) for i in range(ends)]),
            ],
            axis=dim,
        )
    return cells


def vertical_matrix(rows, count):
    cols = jnp.arange(count, dtype=jnp.int32)
    diff = (rows[:, None] - cols[None, :]).astype(jnp.float32)
    return 0.5 * jnp.exp(-diff * diff / (2.0 * vert_scale * vert_scale))


def lat_kernel(widths):
    offsets = jnp.arange(-HALO, HALO + 1, dtype=jnp.int32).astype(jnp.float32)
    spread = widths.astype(jnp.float32)[:, None] / 3.0
    weights = jnp.exp(-offsets[None, :] ** 2 / (2.0 * spread**2))
    norm_sq = jnp.sum(jnp.exp(-offsets[None, :] ** 2 / spread**2), axis=1, keepdims=True)
    return weights / jnp.sqrt(norm_sq)


def lon_table(width, count):
    rows = jnp.arange(count, dtype=jnp.int32)
    diff = jnp.abs(rows[:, None] - rows[None, :])
    dist = jnp.minimum(diff, count - diff).astype(jnp.float32)
    cycle_dist = jnp.minimum(rows, count - rows).astype(jnp.float32)
    scale = width.astype(jnp.float32)
    norm_sq = jnp.sum(jnp.exp(-(cycle_dist**2) / scale**2))
    return (jnp.exp(-(dist**2) / (2.0 * scale**2)) / jnp.sqrt(norm_sq)).astype(jnp.bfloat16)


def lat_apply(padded, kernel, band):
    total = jnp.zeros((padded.shape[0], band, padded.shape[2]), jnp.float32)
    for offset in range(2 * HALO + 1):
        total = total + kernel[:, offset, None, None] * padded[:, offset : offset + band].astype(
            jnp.float32
        )
    return total


def body(alpha_field, perturbation, obs_value, obs_mask, obs_precision, loc_width):
    level_count = alpha_field.shape[1]
    band_rows = alpha_field.shape[2]
    columns = alpha_field.shape[3]
    total_levels = level_count * lax.axis_size("lev")
    level_start = lax.axis_index("lev") * level_count
    mixing = vertical_matrix(level_start + jnp.arange(level_count, dtype=jnp.int32), total_levels)
    kernel = lat_kernel(loc_width)
    tables = jnp.stack([lon_table(loc_width[level], columns) for level in range(level_count)])
    field = alpha_field[0]
    member_pert = perturbation[0]
    rounded = field.astype(jnp.bfloat16)
    gathered = lax.all_gather(rounded, "lev", axis=0, tiled=True)
    vertical = jnp.einsum(
        "ij,jrn->irn", mixing, gathered.astype(jnp.float32), precision=lax.Precision.HIGHEST
    )
    padded = extended(vertical.astype(jnp.bfloat16), (("lat", 1),), HALO)
    smoothed = lat_apply(padded, kernel, band_rows).astype(jnp.bfloat16)
    spread_field = jnp.einsum("lrn,lnm->lrm", smoothed, tables, preferred_element_type=jnp.float32)
    partial_field = member_pert.astype(jnp.float32) * spread_field
    weighted = obs_mask.astype(jnp.float32) * obs_precision[:, None, None]
    increment = lax.psum_scatter(partial_field, "member", scatter_dimension=2, tiled=True)
    adjoint_b = (weighted * (increment - obs_value)).astype(jnp.bfloat16)
    product_b = (
        member_pert.astype(jnp.float32)
        * lax.all_gather(adjoint_b, "member", axis=2, tiled=True).astype(jnp.float32)
    ).astype(jnp.bfloat16)
    along = jnp.einsum("lrn,lnm->lrm", product_b, tables, preferred_element_type=jnp.float32)
    padded_back = extended(along.astype(jnp.bfloat16), (("lat", 1),), HALO)
    smooth_back = lat_apply(padded_back, kernel, band_rows).astype(jnp.bfloat16)
    gathered_back = lax.all_gather(smooth_back, "lev", axis=0, tiled=True)
    gradient = field + jnp.einsum(
        "ij,jrn->irn", mixing, gathered_back.astype(jnp.float32), precision=lax.Precision.HIGHEST
    )
    return (gradient[None], increment)


def solution(mesh):
    return jax.shard_map(
        body,
        mesh=mesh,
        in_specs=(
            P("member", "lev", "lat", None),
            P("member", "lev", "lat", None),
            P("lev", "lat", "member"),
            P("lev", "lat", "member"),
            P("lev"),
            P("lev"),
        ),
        out_specs=(P("member", "lev", "lat", None), P("lev", "lat", "member")),
        check_vma=False,
    )
```

profile of v0, /device:TPU:1, one launch (start us, length us, event | category | flops | bytes accessed | tf_op | source)
XLA Modules:
  0.0 912.6 jit_solution(10440657581060275996)
XLA Ops:
  7.2 2.5 copy.38
  9.7 1.0 copy.17
  10.8 0.7 fusion.128
  12.1 0.6 exponential_reduce_fusion.1
  13.3 0.7 exponential_reduce_fusion
  14.6 0.6 exponential_reduce_fusion.2
  15.9 0.6 exponential_reduce_fusion.3
  19.2 6.2 divide_convert_fusion.2
  25.5 6.2 divide_convert_fusion
  31.9 6.1 all-gather.3.cloned.1.call-done
  38.0 3.1 convolution_convert_fusion
  41.1 1.0 fusion.127
  42.0 2.1 collective-permute-start
  44.1 1.5 collective-permute-start.1
  46.2 0.7 copy.16
  47.0 2.5 collective-permute-done
  49.6 3.7 collective-permute-done.1
  53.3 24.3 %add_convert_fusion.1 = bf16[4,80,1280]{2,0,1:T(4,128)(2,1)S(1)} fusion(bf16[4,80,1280]{2,0,1:T(4,128)(2,1)S(1)} %convolution_convert_fusion, bf16[4,24,1280]{2,0,1:T(4,128)(2,1)S(1)} %collective-permute-done.1, bf16[4,24,1280]{2,0,1:T(4,128)(2,1)S(1)} %collective-permute-done, f32[4]{0:T(128)S(1)} %get-tuple-element.11, f32[4]{0:T(128)S(1)} %get-tuple-element.12, ...), kind=kLoop, calls=%fused_computation.113 | loop fusion | flops 79872000 | bytes 2130704 | tf_op jit(solution)/shard_map/convert_element_type | solution.py:79
  77.6 8.6 convolution_multiply_fusion
  86.3 663.2 %reduce-scatter.2.cloned.1.call-done = f32[4,80,40]{1,2,0:T(8,128)} async-done(((f32[4,80,1280]{1,2,0:T(8,128)}), f32[4,80,40]{1,2,0:T(8,128)}) %reduce-scatter.2.cloned.1.call-update) | async-done | bytes 51216 | tf_op jit(solution)/shard_map/reduce_scatter | solution.py:83
  749.5 1.0 multiply_convert_fusion
  750.5 66.9 %all_gather.10 = bf16[4,80,1280]{1,2,0:T(8,128)(2,1)S(1)} all-gather(bf16[4,80,40]{1,2,0:T(8,128)(2,1)S(1)} %multiply_convert_fusion), channel_id=1, replica_groups=mesh['member'=32,'lat'=8,'lev'=2] {'member'}, dimensions={2}, use_global_device_ids=true | all-gather | bytes 844800 | tf_op jit(solution)/shard_map/all_gather | solution.py:87
  817.4 8.1 fusion.5
  826.2 3.8 collective-permute-start.2
  830.1 1.3 collective-permute-start.3
  831.4 1.8 collective-permute-done.2
  833.2 4.1 collective-permute-done.3
  837.4 23.6 %add_convert_fusion = bf16[4,80,1280]{2,0,1:T(4,128)(2,1)S(1)} fusion(bf16[4,80,1280]{2,0,1:T(4,128)(2,1)S(1)} %copy.37, bf16[4,24,1280]{2,0,1:T(4,128)(2,1)S(1)} %collective-permute-done.3, bf16[4,24,1280]{2,0,1:T(4,128)(2,1)S(1)} %collective-permute-done.2, f32[4]{0:T(128)S(1)} %get-tuple-element.11, f32[4]{0:T(128)S(1)} %get-tuple-element.12, ...), kind=kLoop, calls=%fused_computation.112 | loop fusion | flops 79872000 | bytes 2130704 | tf_op jit(solution)/shard_map/convert_element_type | solution.py:91
  861.0 1.0 copy.23
  862.0 38.7 %all-gather.5.cloned.1.call-done = bf16[8,80,1280]{2,1,0:T(8,128)(2,1)} async-done(((bf16[4,80,1280]{2,1,0:T(8,128)(2,1)}), bf16[8,80,1280]{2,1,0:T(8,128)(2,1)}) %all-gather.5.cloned.1.call-update) | async-done | bytes 1638416 | tf_op jit(solution)/shard_map/all_gather | solution.py:92
  900.7 3.9 fusion.3
  904.6 1.5 copy.25
  (51 shorter events, 1.7 us)
Async XLA Ops:
  7.2 30.8 %all-gather.3.cloned.1.call-start = ((), (), s32[]{:S(2)}) async-start(), calls=%async_computation.1 | async-start | bytes 2457600 | tf_op jit(solution)/shard_map/all_gather | solution.py:74
  9.7 1.1 copy-start.4
  10.7 738.8 %reduce-scatter.2.cloned.1.call-start = ((), (), s32[]{:S(2)}) async-start(), calls=%async_computation.2 | async-start | bytes 2703360 | tf_op jit(solution)/shard_map/reduce_scatter | solution.py:83
  31.8 10.3 %copy-start.14 = (s32[4]{0:T(128)}, s32[4]{0:T(128)S(1)}, u32[]{:S(2)}) copy-start(s32[4]{0:T(128)S(1)} %iota_add_fusion) | copy-start | bytes 52
  31.9 14.4 %copy-start.1 = (bf16[1,4,80,1280]{3,2,1,0:T(8,128)(2,1)S(1)}, bf16[1,4,80,1280]{3,2,1,0:T(8,128)(2,1)}, u32[]{:S(2)}) copy-start(bf16[1,4,80,1280]{3,2,1,0:T(8,128)(2,1)} %param.7) | copy-start | bytes 2457604
  42.0 7.5 collective-permute-start
  44.1 9.1 %collective-permute-start.1 = (bf16[4,24,1280]{2,0,1:T(4,128)(2,1)}, bf16[4,24,1280]{2,0,1:T(4,128)(2,1)S(1)}, u32[]{:S(2)}, u32[]{:S(2)}) collective-permute-start(bf16[4,24,1280]{2,0,1:T(4,128)(2,1)} %get-tuple-element.9), channel_id=1, source_target_pairs={{2,0},{4,2},{6,4},{8,6},{10,8},{12,10},{14,12},{3,1},{5,3},{7,5},{... | collective-permute-start | bytes 737288 | tf_op jit(solution)/shard_map/ppermute | solution.py:22
  86.2 663.3 %copy-start.2 = (f32[4,80,40]{1,2,0:T(8,128)S(1)}, f32[4,80,40]{1,2,0:T(8,128)}, u32[]{:S(2)}) copy-start(f32[4,80,40]{1,2,0:T(8,128)} %param.8) | copy-start | bytes 153604
  86.2 663.3 %copy-start.3 = (s32[4,80,40]{1,2,0:T(8,128)S(1)}, s32[4,80,40]{1,2,0:T(8,128)}, u32[]{:S(2)}) copy-start(s32[4,80,40]{1,2,0:T(8,128)} %param.9) | copy-start | bytes 153604
  86.2 663.3 %copy-start.16 = (f32[4]{0:T(128)S(1)}, f32[4]{0:T(128)}, u32[]{:S(2)}) copy-start(f32[4]{0:T(128)} %param.10) | copy-start | bytes 52
  86.2 814.5 %all-gather.5.cloned.1.call-start = ((), (), s32[]{:S(2)}) async-start(), calls=%async_computation.3 | async-start | bytes 2457600 | tf_op jit(solution)/shard_map/all_gather | solution.py:92
  825.5 11.8 %copy-start.5 = (f32[4]{0:T(128)S(1)}, f32[4]{0:T(128)}, u32[]{:S(2)}) copy-start(f32[4]{0:T(128)} %get-tuple-element.50) | copy-start | bytes 52
  825.5 11.8 %copy-start.6 = (f32[4]{0:T(128)S(1)}, f32[4]{0:T(128)}, u32[]{:S(2)}) copy-start(f32[4]{0:T(128)} %get-tuple-element.51) | copy-start | bytes 52
  825.5 11.8 %copy-start.7 = (f32[4]{0:T(128)S(1)}, f32[4]{0:T(128)}, u32[]{:S(2)}) copy-start(f32[4]{0:T(128)} %get-tuple-element.52) | copy-start | bytes 52
  825.5 11.8 %copy-start.8 = (f32[4]{0:T(128)S(1)}, f32[4]{0:T(128)}, u32[]{:S(2)}) copy-start(f32[4]{0:T(128)} %get-tuple-element.53) | copy-start | bytes 52
  825.5 11.8 %copy-start.9 = (f32[4]{0:T(128)S(1)}, f32[4]{0:T(128)}, u32[]{:S(2)}) copy-start(f32[4]{0:T(128)} %get-tuple-element.54) | copy-start | bytes 52
  825.6 11.8 %copy-start.10 = (f32[4]{0:T(128)S(1)}, f32[4]{0:T(128)}, u32[]{:S(2)}) copy-start(f32[4]{0:T(128)} %get-tuple-element.55) | copy-start | bytes 52
  825.6 11.8 %copy-start.11 = (f32[4]{0:T(128)S(1)}, f32[4]{0:T(128)}, u32[]{:S(2)}) copy-start(f32[4]{0:T(128)} %get-tuple-element.56) | copy-start | bytes 52
  825.6 11.8 %copy-start.12 = (f32[4]{0:T(128)S(1)}, f32[4]{0:T(128)}, u32[]{:S(2)}) copy-start(f32[4]{0:T(128)} %get-tuple-element.57) | copy-start | bytes 52
  825.6 11.8 %copy-start.13 = (f32[4]{0:T(128)S(1)}, f32[4]{0:T(128)}, u32[]{:S(2)}) copy-start(f32[4]{0:T(128)} %get-tuple-element.58) | copy-start | bytes 52
  826.2 7.0 collective-permute-start.2
  830.1 7.2 collective-permute-start.3
  861.0 39.7 %copy-start = (f32[1,4,80,1280]{3,2,1,0:T(8,128)S(1)}, f32[1,4,80,1280]{3,2,1,0:T(8,128)}, u32[]{:S(2)}) copy-start(f32[1,4,80,1280]{3,2,1,0:T(8,128)} %param.6) | copy-start | bytes 4915204
  861.0 39.7 %copy-start.15 = (s32[4]{0:T(128)S(1)}, s32[4]{0:T(128)}, u32[]{:S(2)}) copy-start(s32[4]{0:T(128)} %copy-done.14) | copy-start | bytes 52
Sparse Core Ops, SparseCore 0:
  10.8 27.1 all-gather.2
  86.4 663.1 reduce-scatter.1
  862.1 38.5 all-gather.4
where the time goes:
time: 913 us
  waiting for transfers between devices  720 us (79%)
  blocking collectives  66.9 us (7%)
  other arithmetic  64 us (7%)
  matrix products  23.7 us (3%)
  between operations  19.3 us (2%)
  local copies, waits for them, and re-layouts  9.59 us (1%)
    reduce_scatter x1, waiting for transfers between devices, body(): lax.psum_scatter(partial_field, 'member', scatter_dimension=2, tiled=True)  663 us
    all_gather x1, blocking collectives, body(): lax.all_gather(adjoint_b, 'member', axis=2, tiled=True).astype(jnp.float32)  66.9 us
    all_gather x1, waiting for transfers between devices, body(): gathered_back = lax.all_gather(smooth_back, 'lev', axis=0, tiled=True)  38.7 us
    convert_element_type x1, other arithmetic, body(): smoothed = lat_apply(padded, kernel, band_rows).astype(jnp.bfloat16)  24.3 us
    convert_element_type x1, other arithmetic, body(): smooth_back = lat_apply(padded_back, kernel, band_rows).astype(jnp.bfloat16)  23.6 us
  transfers between devices with their start and end apart: 7, of which 7 were waited for; matrix products, arithmetic and copies ran while one was open for 2% of the time, Pallas kernels for 0%

commit v1 on v0

v1 whole, which is shorter than its diff:
```python
import functools
import math

import jax
import jax.numpy as jnp
from jax import lax
from jax.experimental import pallas as pl
from jax.experimental.pallas import tpu as pltpu
from jax.sharding import PartitionSpec as P

HALO = 24
GROUPS = 2
BLOCK = 256
VERT_SCALE = 2.0
F32 = jnp.float32
BF16 = jnp.bfloat16
MESH = pl.DeviceIdType.MESH


def vert_weight(diff):
    return 0.5 * math.exp(-diff * diff / (2.0 * VERT_SCALE * VERT_SCALE))


def kernel(
    ring, lat_count, lev_count,
    alpha, pert, obs, mask, prec, width,
    grad, inc,
    own, far, band, edge_f, edge, halo, latk, table, rolled, flat, turned,
    run_tx, run_rx, pair_tx, pair_rx, site, total, adj, back, back_far,
    lev_send, lev_recv, halo_send, halo_recv, site_send, site_recv,
    run_send, run_recv, pair_send, pair_recv, gather_send, gather_recv,
):
    levels, rows, cols = alpha.shape
    blocks = cols // BLOCK
    cell = cols // (ring * GROUPS)
    half = ring // 2
    pad = flat.shape[0]
    used = levels * rows

    member = lax.axis_index("member")
    lat = lax.axis_index("lat")
    lev = lax.axis_index("lev")
    z = lax.rem(member, ring)
    group = lax.div(member, ring)

    def at_z(index):
        return {"member": group * ring + lax.rem(index + ring, ring)}

    after, before = at_z(z + 1), at_z(z - 1)
    pair = {"member": lax.rem(member + ring, ring * GROUPS)}
    south = {"lat": lax.rem(lat + 1, lat_count)}
    north = {"lat": lax.rem(lat + lat_count - 1, lat_count)}
    sibling = {"lev": 1 - lev}

    def remote(src, dst, send, recv, to):
        return pltpu.make_async_remote_copy(
            src_ref=src, dst_ref=dst, send_sem=send, recv_sem=recv, device_id=to, device_id_type=MESH
        )

    def lev_copy(phase, level):
        src, dst = ((own, far), (back, back_far))[phase]
        return remote(src.at[level], dst.at[level], lev_send.at[phase, level], lev_recv.at[phase, level], sibling)

    def halo_copy(phase, side):
        return remote(
            edge.at[phase, side], halo.at[phase, 1 - side],
            halo_send.at[phase, side], halo_recv.at[phase, 1 - side], (north, south)[side],
        )

    def site_copy():
        return remote(site.at[group], site.at[group], site_send, site_recv, pair)

    def site_arrival():
        return remote(site.at[1 - group], site.at[1 - group], site_send, site_recv, pair)

    def run_copy(way, step):
        return remote(
            run_tx.at[way, step], run_rx.at[way, step],
            run_send.at[way, step], run_recv.at[way, step], (after, before)[way],
        )

    def pair_copy():
        return remote(pair_tx, pair_rx, pair_send, pair_recv, pair)

    def origin(way, step):
        return lax.rem(z + (ring - step if way == 0 else step), ring)

    def gather_copy(way, step):
        chunk = origin(way, step)
        return remote(
            adj.at[chunk], adj.at[chunk], gather_send.at[way, step], gather_recv.at[way, step], (after, before)[way]
        )

    def gather_arrival(way, step):
        chunk = origin(way, step + 1)
        return remote(
            adj.at[chunk], adj.at[chunk], gather_send.at[way, step], gather_recv.at[way, step], (after, before)[way]
        )

    barrier = pltpu.get_barrier_semaphore()
    partners = (after, before, pair, south, north, sibling)
    for partner in partners:
        pl.semaphore_signal(barrier, inc=1, device_id=partner, device_id_type=MESH)

    def round_level(level, carry):
        own[level] = alpha[level].astype(BF16)
        return carry

    lax.fori_loop(0, levels, round_level, 0)

    site[group] = jnp.zeros(site.shape[1:], F32)
    for level in range(levels):
        lanes = slice(level * rows, (level + 1) * rows)
        site[group, 0, :, lanes] = obs[level]
        site[group, 1, :, lanes] = mask[level].astype(F32) * prec[level]
    pl.semaphore_wait(barrier, len(partners))

    for level in range(levels):
        lev_copy(0, level).start()
    site_copy().start()

    def build_latk(level, carry):
        scale = jnp.full((1, 128), width[level].astype(F32), F32) / 3.0
        lane = lax.broadcasted_iota(jnp.int32, (1, 128), 1)
        step = (lane - HALO).astype(F32)
        norm_sq = jnp.sum(
            jnp.where(lane <= 2 * HALO, jnp.exp(-(step * step) / (scale * scale)), 0.0), axis=1, keepdims=True
        )
        row = lax.broadcasted_iota(jnp.int32, (rows, 128), 0)
        col = lax.broadcasted_iota(jnp.int32, (rows, 128), 1)
        is_top = jnp.logical_and(col >= rows, col < rows + HALO)
        is_bottom = col >= rows + HALO
        place = jnp.where(is_top, col - rows - HALO, col)
        place = jnp.where(is_bottom, col - HALO, place)
        diff = place - row
        keep = jnp.abs(diff) <= HALO
        keep = jnp.logical_and(keep, jnp.logical_or(jnp.logical_not(is_top), lat > 0))
        keep = jnp.logical_and(keep, jnp.logical_or(jnp.logical_not(is_bottom), lat < lat_count - 1))
        dist = diff.astype(F32)
        weight = jnp.exp(-(dist * dist) / (2.0 * scale * scale)) / jnp.sqrt(norm_sq)
        weight = jnp.where(keep, weight, 0.0)
        high = weight.astype(BF16)
        latk[level, 0:rows] = high
        latk[level, rows : 2 * rows] = (weight - high.astype(F32)).astype(BF16)
        return carry

    lax.fori_loop(0, levels, build_latk, 0)

    def build_table(level, carry):
        scale = jnp.full((1, 128), width[level].astype(F32), F32)[:, 0:1]
        square = scale * scale
        place = lax.broadcasted_iota(jnp.int32, (1, cols), 1)
        cycle = jnp.minimum(place, cols - place).astype(F32)
        norm_sq = jnp.sum(jnp.exp(-(cycle * cycle) / square), axis=1, keepdims=True)
        inverse = 1.0 / jnp.sqrt(norm_sq)
        factor = -1.0 / (2.0 * square)
        chunk = 64

        def some(index, inner):
            row = lax.broadcasted_iota(jnp.int32, (chunk, BLOCK), 0) + index * chunk
            col = lax.broadcasted_iota(jnp.int32, (chunk, BLOCK), 1)
            diff = jnp.abs(row - col)
            dist = jnp.minimum(diff, cols - diff).astype(F32)
            table[level, pl.ds(pl.multiple_of(index * chunk, chunk), chunk)] = (
                jnp.exp(dist * dist * factor) * inverse
            ).astype(BF16)
            return inner

        return lax.fori_loop(0, cols // chunk, some, carry)

    near_weights = [[vert_weight(i - j) for j in range(levels)] for i in range(levels)]
    far_weights = [
        [
            jnp.where(lev == 0, jnp.float32(vert_weight(i - j - levels)), jnp.float32(vert_weight(i - j + levels)))
            for j in range(levels)
        ]
        for i in range(levels)
    ]

    def vertical(near, remote_levels, emit):
        def lane_block(block, carry):
            lanes = pl.ds(pl.multiple_of(block * BLOCK, BLOCK), BLOCK)
            for chunk in range(rows // 16):
                part = slice(16 * chunk, 16 * chunk + 16)
                a = [near[j, part, lanes].astype(F32) for j in range(levels)]
                b = [remote_levels[j, part, lanes].astype(F32) for j in range(levels)]
                for i in range(levels):
                    value = near_weights[i][0] * a[0]
                    for j in range(1, levels):
                        value = value + near_weights[i][j] * a[j]
                    for j in range(levels):
                        value = value + far_weights[i][j] * b[j]
                    emit(i, chunk, part, lanes, value)
            return carry

        lax.fori_loop(0, blocks, lane_block, 0)

    def emit_forward(i, chunk, part, lanes, value):
        band[i, part, lanes] = value.astype(BF16)
        first = 16 * chunk
        top = min(HALO, first + 16) - first
        if top > 0:
            edge_f[0, HALO * i + first : HALO * i + first + top, lanes] = value[0:top]
        skip = max(0, rows - HALO - first)
        if skip < 16:
            start = HALO * i + first + skip - (rows - HALO)
            edge_f[1, start : start + 16 - skip, lanes] = value[skip:16]

    for level in range(levels):
        lev_copy(0, level).wait_recv()
    vertical(own, far, emit_forward)

    def send_edges(phase):
        def lane_block(block, carry):
            lanes = pl.ds(pl.multiple_of(block * BLOCK, BLOCK), BLOCK)
            for side in range(2):
                edge[phase, side, :, lanes] = edge_f[side, :, lanes].astype(BF16)
            return carry

        lax.fori_loop(0, blocks, lane_block, 0)
        for side in range(2):
            halo_copy(phase, side).start()

    def receive_edges(phase):
        for side in range(2):
            halo_copy(phase, side).wait_recv()

        def lane_block(block, carry):
            lanes = pl.ds(pl.multiple_of(block * BLOCK, BLOCK), BLOCK)
            top = halo[phase, 0, :, lanes].astype(F32)
            bottom = halo[phase, 1, :, lanes].astype(F32)
            for i in range(levels):
                part = slice(HALO * i, HALO * i + HALO)
                band[i, rows : rows + 2 * HALO, lanes] = jnp.concatenate([top[part], bottom[part]], axis=0).astype(BF16)
            return carry

        lax.fori_loop(0, blocks, lane_block, 0)

    def smooth(level, block):
        both = jnp.dot(latk[level], band[level, :, block * BLOCK : (block + 1) * BLOCK], preferred_element_type=F32)
        return (both[0:rows] + both[rows : 2 * rows]).astype(BF16)

    def spread_out(block, value):
        for turn in range(blocks):
            start = ((block - turn) % blocks) * BLOCK
            rolled[turn * rows : (turn + 1) * rows, start : start + BLOCK] = value

    def along_longitude(level):
        return jnp.dot(rolled[...], table[level], preferred_element_type=F32)

    send_edges(0)
    lax.fori_loop(0, levels, build_table, 0)
    flat[used:pad] = jnp.zeros((pad - used, cols), F32)
    receive_edges(0)

    def forward(level, carry):
        for block in range(blocks):
            spread_out(block, smooth(level, block))
        out = along_longitude(level)
        here = pl.ds(pl.multiple_of(level * rows, 16), rows)
        for block in range(blocks):
            lanes = slice(block * BLOCK, (block + 1) * BLOCK)
            flat[here, lanes] = out[block * rows : (block + 1) * rows] * pert[level, :, lanes].astype(F32)
        return carry

    lax.fori_loop(0, levels, forward, 0)

    def turn_forward(index, carry):
        part = pl.ds(pl.multiple_of(index * 128, 128), 128)
        turned[part, :] = flat[:, part].T
        return carry

    lax.fori_loop(0, cols // 128, turn_forward, 0)

    def split_rows(chunk):
        return [pl.ds(pl.multiple_of(g * (cols // GROUPS) + chunk * cell, 8), cell) for g in range(GROUPS)]

    def term(chunk):
        return jnp.concatenate([turned[part, :] for part in split_rows(chunk)], axis=0)

    def target(way, step):
        return lax.rem(z + (half - step if way == 0 else half + 1 + step), ring)

    for way in range(2):
        run_tx[way, 0] = term(target(way, 0)).astype(BF16)
        run_copy(way, 0).start()

    def hop(way, step):
        run_copy(way, step - 1).wait_recv()
        run_tx[way, step] = (run_rx[way, step - 1].astype(F32) + term(target(way, step))).astype(BF16)
        run_copy(way, step).start()

    def hops(step, carry):
        for way in range(2):
            hop(way, step)
        return carry

    lax.fori_loop(1, half - 1, hops, 0)
    hop(0, half - 1)
    run_copy(1, half - 2).wait_recv()
    mine = term(z) + run_rx[1, half - 2].astype(F32)
    run_copy(0, half - 1).wait_recv()
    mine = mine + run_rx[0, half - 1].astype(F32)
    total[...] = mine
    pair_tx[...] = mine.astype(BF16)
    pair_copy().start()
    site_arrival().wait_recv()
    pair_copy().wait_recv()
    summed = total[...] + pair_rx[...].astype(F32)
    total[...] = summed
    seen = jnp.concatenate([site[g, 0] for g in range(GROUPS)], axis=0)
    weight = jnp.concatenate([site[g, 1] for g in range(GROUPS)], axis=0)
    adj[z] = (weight * (summed - seen)).astype(BF16)

    for way in range(2):
        gather_copy(way, 0).start()

    def unpack(chunk):
        value = adj[chunk].astype(F32)
        for g, part in enumerate(split_rows(chunk)):
            turned[part, :] = value[g * cell : (g + 1) * cell]

    unpack(z)
    result = total[pl.ds(pl.multiple_of(group * cell, 8), cell), :]
    for level in range(levels):
        inc[level] = result[:, level * rows : (level + 1) * rows]

    def pass_on(way, step):
        gather_arrival(way, step - 1).wait_recv()
        gather_copy(way, step).start()
        unpack(origin(way, step))

    def passes(step, carry):
        for way in range(2):
            pass_on(way, step)
        return carry

    lax.fori_loop(1, half - 1, passes, 0)
    pass_on(0, half - 1)
    gather_arrival(1, half - 2).wait_recv()
    unpack(origin(1, half - 1))
    gather_arrival(0, half - 1).wait_recv()
    unpack(origin(0, half))

    def turn_back(index, carry):
        part = pl.ds(pl.multiple_of(index * 128, 128), 128)
        flat[:, part] = turned[part, :].T
        return carry

    lax.fori_loop(0, cols // 128, turn_back, 0)

    def backward(level, carry):
        here = pl.ds(pl.multiple_of(level * rows, 16), rows)
        for block in range(blocks):
            lanes = slice(block * BLOCK, (block + 1) * BLOCK)
            spread_out(block, (flat[here, lanes] * pert[level, :, lanes].astype(F32)).astype(BF16))
        out = along_longitude(level)
        reach = pl.ds(pl.multiple_of(level * HALO, 8), HALO)
        for block in range(blocks):
            lanes = slice(block * BLOCK, (block + 1) * BLOCK)
            value = out[block * rows : (block + 1) * rows]
            band[level, 0:rows, lanes] = value.astype(BF16)
            edge_f[0, reach, lanes] = value[0:HALO]
            edge_f[1, reach, lanes] = value[rows - HALO : rows]
        return carry

    lax.fori_loop(0, levels, backward, 0)
    send_edges(1)
    receive_edges(1)

    def smooth_back(level, carry):
        for block in range(blocks):
            back[level, :, block * BLOCK : (block + 1) * BLOCK] = smooth(level, block)
        lev_copy(1, level).start()
        return carry

    lax.fori_loop(0, levels, smooth_back, 0)

    def emit_back(i, chunk, part, lanes, value):
        grad[i, part, lanes] = alpha[i, part, lanes] + value

    for level in range(levels):
        lev_copy(1, level).wait_recv()
    vertical(back, back_far, emit_back)

    for phase in range(2):
        for level in range(levels):
            lev_copy(phase, level).wait_send()
        for side in range(2):
            halo_copy(phase, side).wait_send()
    site_copy().wait_send()
    pair_copy().wait_send()

    def drain(step, carry):
        for way in range(2):
            run_copy(way, step).wait_send()
            gather_copy(way, step).wait_send()
        return carry

    lax.fori_loop(0, half - 1, drain, 0)
    run_copy(0, half - 1).wait_send()
    gather_copy(0, half - 1).wait_send()


def solution(mesh):
    ring = mesh.shape["member"] // GROUPS
    lat_count, lev_count = mesh.shape["lat"], mesh.shape["lev"]

    def body(alpha_field, perturbation, obs_value, obs_mask, obs_precision, loc_width):
        _, levels, rows, cols = alpha_field.shape
        cell = obs_value.shape[2]
        used = levels * rows
        pad = -(-used // 128) * 128
        chunk = GROUPS * cell
        half = ring // 2
        vmem = pl.BlockSpec(memory_space=pltpu.VMEM)
        smem = pl.BlockSpec(memory_space=pltpu.SMEM)
        dma = pltpu.SemaphoreType.DMA
        full = (levels, rows, cols)
        gradient, increment = pl.pallas_call(
            functools.partial(kernel, ring, lat_count, lev_count),
            out_shape=(
                jax.ShapeDtypeStruct(full, F32),
                jax.ShapeDtypeStruct((levels, cell, rows), F32),
            ),
            in_specs=[vmem, vmem, vmem, vmem, smem, smem],
            out_specs=(vmem, vmem),
            scratch_shapes=[
                pltpu.VMEM(full, BF16),
                pltpu.VMEM(full, BF16),
                pltpu.VMEM((levels, rows + 2 * HALO, cols), BF16),
                pltpu.VMEM((2, levels * HALO, cols), F32),
                pltpu.VMEM((2, 2, levels * HALO, cols), BF16),
                pltpu.VMEM((2, 2, levels * HALO, cols), BF16),
                pltpu.VMEM((levels, 2 * rows, rows + 2 * HALO), BF16),
                pltpu.VMEM((levels, cols, BLOCK), BF16),
                pltpu.VMEM((cols // BLOCK * rows, cols), BF16),
                pltpu.VMEM((pad, cols), F32),
                pltpu.VMEM((cols, pad), F32),
                pltpu.VMEM((2, half, chunk, pad), BF16),
                pltpu.VMEM((2, half, chunk, pad), BF16),
                pltpu.VMEM((chunk, pad), BF16),
                pltpu.VMEM((chunk, pad), BF16),
                pltpu.VMEM((GROUPS, 2, cell, pad), F32),
                pltpu.VMEM((chunk, pad), F32),
                pltpu.VMEM((ring, chunk, pad), BF16),
                pltpu.VMEM(full, BF16),
                pltpu.VMEM(full, BF16),
                dma((2, levels)), dma((2, levels)),
                dma((2, 2)), dma((2, 2)),
                dma, dma,
                dma((2, half)), dma((2, half)),
                dma, dma,
                dma((2, half)), dma((2, half)),
            ],
            compiler_params=pltpu.CompilerParams(
                collective_id=0, has_side_effects=True, vmem_limit_bytes=56 * 1024 * 1024
            ),
            name="envar",
        )(
            alpha_field[0],
            perturbation[0],
            obs_value.transpose(0, 2, 1),
            obs_mask.transpose(0, 2, 1),
            obs_precision,
            loc_width,
        )
        return gradient[None], increment.transpose(0, 2, 1)

    return jax.shard_map(
        body,
        mesh=mesh,
        in_specs=(
            P("member", "lev", "lat", None),
            P("member", "lev", "lat", None),
            P("lev", "lat", "member"),
            P("lev", "lat", "member"),
            P("lev"),
            P("lev"),
        ),
        out_specs=(P("member", "lev", "lat", None), P("lev", "lat", "member")),
        check_vma=False,
    )
```

time: 913 us -> 109 us (0.12)
  waiting for transfers between devices: 720 us -> 0 us
  Pallas kernels: 0 us -> 104 us
  blocking collectives: 66.9 us -> 0 us
  other arithmetic: 64 us -> 0 us
  matrix products: 23.7 us -> 0 us
  between operations: 19.3 us -> 0.65 us
    reduce_scatter x1 -> x0, waiting for transfers between devices: 663 us -> none  [body(): lax.psum_scatter(partial_field, 'member', scatter_dimension=2, tiled=True)]
    pallas_call x0 -> x1, Pallas kernels: none -> 104 us  [body(): pl.pallas_call(functools.partial(kernel, ring, lat_count, lev_count), out...]
    all_gather x1 -> x0, blocking collectives: 66.9 us -> none  [body(): lax.all_gather(adjoint_b, 'member', axis=2, tiled=True).astype(jnp.float32)]
    convert_element_type x5 -> x0, other arithmetic: 61.3 us -> none  [the longest x1 24.3 us: body(): smoothed = lat_apply(padded, kernel, band_rows).astype(jnp.bfloat16)]
    all_gather x2 -> x0, waiting for transfers between devices: 44.8 us -> none  [the longest x1 38.7 us: body(): gathered_back = lax.all_gather(smooth_back, 'lev', axis=0, tiled=True)]
    dot_general x4 -> x0, matrix products: 23.7 us -> none  [the longest x1 8.63 us: body(): jnp.einsum('lrn,lnm->lrm', smoothed, tables, preferred_element_type=jnp.f...]
    ppermute x4 -> x0, waiting for transfers between devices: 12.2 us -> none  [the longest x2 7.83 us: extended(): lax.ppermute(head, axis, [((i + 1) % count, i) for i in range(ends)])]
  transfers between devices with their start and end apart: 7 -> 0, of which waited for: 7 -> 0; matrix products, arithmetic and copies ran while one was open for 2% -> 0% of each run, Pallas kernels for 0% -> 0%
where the time goes in v1:
time: 109 us; the launch traced here: 108 us
  Pallas kernels  104 us (95%)
  local copies, waits for them, and re-layouts  3.42 us (3%)
    pallas_call x1, Pallas kernels, body(): pl.pallas_call(functools.partial(kernel, ring, lat_count, lev_count), out...  104 us
    unnamed x4, local copies, waits for them, and re-layouts  3.42 us

profile of v1, /device:TPU:1, one launch (start us, length us, event | category | flops | bytes accessed | tf_op | source)
XLA Modules:
  0.0 108.4 jit_solution(14586984571835606807)
XLA Ops:
  0.6 104.3 %envar.1 = (f32[4,80,1280]{2,1,0:T(8,128)}, f32[4,40,80]{2,1,0:T(8,128)}) custom-call(f32[4,80,1280]{2,1,0:T(8,128)} %bitcast.6, bf16[4,80,1280]{2,1,0:T(8,128)(2,1)} %bitcast.8, f32[4,40,80]{2,1,0:T(8,128)} %bitcast.9, s32[4,40,80]{2,1,0:T(8,128)} %bitcast.10, f32[4]{0:T(128)} %prec.1, s32[4]{0:T(128)} %width.1), custom_call_target="tpu_custom_call" | custom-call | tf_op jit(solution)/shard_map/envar/pallas_call | solution.py:420
  105.0 0.0 copy-start
  105.0 2.8 %copy.10 = f32[1,4,80,1280]{3,2,1,0:T(8,128)} copy(f32[1,4,80,1280]{3,2,1,0:T(8,128)} %bitcast.7) | data formatting | bytes 3276800
  107.8 0.0 copy-done
  107.8 0.6 copy.11
Async XLA Ops:
  105.0 2.8 %copy-start = (f32[4,40,80]{2,1,0:T(8,128)S(1)}, f32[4,40,80]{2,1,0:T(8,128)}, u32[]{:S(2)}) copy-start(f32[4,40,80]{2,1,0:T(8,128)} %get-tuple-element.5) | copy-start | bytes 153604

commit v2 on v0

v2 whole, which is shorter than its diff:
```python
import functools
import math

import jax
import jax.numpy as jnp
from jax import lax
from jax.experimental import pallas as pl
from jax.experimental.pallas import tpu as pltpu
from jax.sharding import PartitionSpec as P

HALO = 24
GROUPS = 2
PAIRS = 2
BLOCK = 256
VERT_SCALE = 2.0
F32 = jnp.float32
BF16 = jnp.bfloat16
MESH = pl.DeviceIdType.MESH

SIDE = [(0, 3), (3, 6), (3, 4), (3, 2), (6, 8), (6, 7), (4, 5), (2, 1)]
TREE = SIDE + [(-p, -c) for p, c in SIDE if c < 8]


def tree_depth(node):
    return 0 if node == 0 else 1 + tree_depth(next(p for p, c in TREE if c == node))


def round_up(value, to):
    return -(-value // to) * to


def vert_weight(diff):
    return 0.5 * math.exp(-diff * diff / (2.0 * VERT_SCALE * VERT_SCALE))


def vert_weights(lev, levels):
    near = [[vert_weight(i - j) for j in range(levels)] for i in range(levels)]
    far = [
        [
            jnp.where(lev == 0, jnp.float32(vert_weight(i - j - levels)), jnp.float32(vert_weight(i - j + levels)))
            for j in range(levels)
        ]
        for i in range(levels)
    ]
    return near, far


def mix(near, far, a, b, i):
    value = near[i][0] * a[0]
    for j in range(1, len(a)):
        value = value + near[i][j] * a[j]
    for j in range(len(b)):
        value = value + far[i][j] * b[j]
    return value


def remainder_rows(chunk):
    return round_up(-(-chunk // 4), 8)


def packed_rows(chunk):
    return round_up(chunk + remainder_rows(chunk), 16)


def pack(value):
    chunk = value.shape[0]
    part = remainder_rows(chunk)
    rest = value[:, 128:256]
    tail = rest[0:part]
    for g in range(1, 4):
        piece = rest[g * part : min((g + 1) * part, chunk)]
        if piece.shape[0] == 0:
            continue
        if piece.shape[0] < part:
            piece = jnp.concatenate([piece, jnp.zeros((part - piece.shape[0], 128), value.dtype)], axis=0)
        tail = tail + pltpu.roll(piece, 32 * g, 1)
    parts = [value[:, 0:128], tail]
    left = packed_rows(chunk) - chunk - part
    if left:
        parts.append(jnp.zeros((left, 128), value.dtype))
    return jnp.concatenate(parts, axis=0)


def unpack(value, chunk):
    part = remainder_rows(chunk)
    tail = value[chunk : chunk + part]
    pieces = [tail]
    for g in range(1, 4):
        keep = min(part, chunk - g * part)
        if keep > 0:
            pieces.append(pltpu.roll(tail, 128 - 32 * g, 1)[0:keep])
    return jnp.concatenate([value[0:chunk], jnp.concatenate(pieces, axis=0)], axis=1)


def kernel(
    ring, lat_count, lev_count,
    alpha, pert, obs, mask, prec, width,
    back_out, far_out, inc,
    own, far, band, edge_f, edge, halo, latk, table, rolled, flat, turned,
    terms, sum_tx, sum_rx, pair_tx, pair_rx, site, total, seen, adj, back,
    lev_send, lev_recv, halo_send, halo_recv, site_send, site_recv,
    sum_send, sum_recv, pair_send, pair_recv, gather_send, gather_recv, out_sem,
):
    levels, rows, cols = alpha.shape
    blocks = cols // BLOCK
    cell = cols // (ring * GROUPS)
    chunk_rows = GROUPS * cell
    pad = flat.shape[0]
    deep = levels // PAIRS
    used = deep * rows
    nodes = [0] + [c for _, c in TREE]
    index = {c: i for i, (_, c) in enumerate(TREE)}
    parent = {c: p for p, c in TREE}
    children = {n: [c for p, c in TREE if p == n] for n in nodes}
    depth = {n: tree_depth(n) for n in nodes}
    height = {}
    for n in sorted(nodes, key=lambda n: -depth[n]):
        height[n] = 1 + max([height[c] for c in children[n]], default=-1)

    member = lax.axis_index("member")
    lat = lax.axis_index("lat")
    lev = lax.axis_index("lev")
    z = lax.rem(member, ring)
    group = lax.div(member, ring)

    def place(offset):
        return lax.rem(z + (ring + offset), ring)

    def at(offset):
        return {"member": group * ring + place(offset)}

    pair = {"member": lax.rem(member + ring, ring * GROUPS)}
    south = {"lat": lax.rem(lat + 1, lat_count)}
    north = {"lat": lax.rem(lat + lat_count - 1, lat_count)}
    sibling = {"lev": 1 - lev}

    def remote(src, dst, send, recv, to):
        return pltpu.make_async_remote_copy(
            src_ref=src, dst_ref=dst, send_sem=send, recv_sem=recv, device_id=to, device_id_type=MESH
        )

    def lev_copy(phase, level):
        src, dst = ((own, far), (back, far_out))[phase]
        return remote(src.at[level], dst.at[level], lev_send.at[phase, level], lev_recv.at[phase, level], sibling)

    def halo_copy(phase, h, side):
        return remote(
            edge.at[phase, h, side], halo.at[phase, h, 1 - side],
            halo_send.at[phase, h, side], halo_recv.at[phase, h, 1 - side], (north, south)[side],
        )

    def site_copy(whose):
        return remote(site.at[whose], site.at[whose], site_send, site_recv, pair)

    def sum_copy(h, node):
        i = index[node]
        to = at(parent[node] - node)
        return remote(sum_tx.at[h, i], sum_rx.at[h, i], sum_send.at[h, i], sum_recv.at[h, i], to)

    def pair_copy(h):
        return remote(pair_tx.at[h], pair_rx.at[h], pair_send.at[h], pair_recv.at[h], pair)

    def gather_copy(h, node, holder):
        i = index[node]
        chunk = place(-holder)
        to = at(node - parent[node])
        return remote(adj.at[h, chunk], adj.at[h, chunk], gather_send.at[h, i], gather_recv.at[h, i], to)

    barrier = pltpu.get_barrier_semaphore()
    jumps = sorted({p - c for p, c in TREE} | {c - p for p, c in TREE})
    partners = [sibling, south, north, pair] + [at(jump) for jump in jumps]
    for partner in partners:
        pl.semaphore_signal(barrier, inc=1, device_id=partner, device_id_type=MESH)

    def round_level(level, carry):
        own[level] = alpha[level].astype(BF16)
        return carry

    lax.fori_loop(0, levels, round_level, 0)

    site[group] = jnp.zeros(site.shape[1:], F32)
    for level in range(levels):
        lanes = slice((level % deep) * rows, (level % deep + 1) * rows)
        site[group, level // deep, 0, :, lanes] = obs[level]
        site[group, level // deep, 1, :, lanes] = mask[level].astype(F32) * prec[level]

    def build_latk(level, carry):
        scale = jnp.full((1, 128), width[level].astype(F32), F32) / 3.0
        lane = lax.broadcasted_iota(jnp.int32, (1, 128), 1)
        step = (lane - HALO).astype(F32)
        norm_sq = jnp.sum(
            jnp.where(lane <= 2 * HALO, jnp.exp(-(step * step) / (scale * scale)), 0.0), axis=1, keepdims=True
        )
        row = lax.broadcasted_iota(jnp.int32, (rows, 128), 0)
        col = lax.broadcasted_iota(jnp.int32, (rows, 128), 1)
        is_top = jnp.logical_and(col >= rows, col < rows + HALO)
        is_bottom = col >= rows + HALO
        spot = jnp.where(is_top, col - rows - HALO, col)
        spot = jnp.where(is_bottom, col - HALO, spot)
        diff = spot - row
        keep = jnp.abs(diff) <= HALO
        keep = jnp.logical_and(keep, jnp.logical_or(jnp.logical_not(is_top), lat > 0))
        keep = jnp.logical_and(keep, jnp.logical_or(jnp.logical_not(is_bottom), lat < lat_count - 1))
        dist = diff.astype(F32)
        weight = jnp.exp(-(dist * dist) / (2.0 * scale * scale)) / jnp.sqrt(norm_sq)
        weight = jnp.where(keep, weight, 0.0)
        high = weight.astype(BF16)
        latk[level, 0:rows] = high
        latk[level, rows : 2 * rows] = (weight - high.astype(F32)).astype(BF16)
        return carry

    lax.fori_loop(0, levels, build_latk, 0)

    def build_table(level, carry):
        scale = jnp.full((1, 128), width[level].astype(F32), F32)[:, 0:1]
        square = scale * scale
        spot = lax.broadcasted_iota(jnp.int32, (1, cols), 1)
        cycle = jnp.minimum(spot, cols - spot).astype(F32)
        norm_sq = jnp.sum(jnp.exp(-(cycle * cycle) / square), axis=1, keepdims=True)
        inverse = 1.0 / jnp.sqrt(norm_sq)
        factor = -1.0 / (2.0 * square)
        step = 64

        def some(i, inner):
            row = lax.broadcasted_iota(jnp.int32, (step, BLOCK), 0) + i * step
            col = lax.broadcasted_iota(jnp.int32, (step, BLOCK), 1)
            diff = jnp.abs(row - col)
            dist = jnp.minimum(diff, cols - diff).astype(F32)
            table[level, pl.ds(pl.multiple_of(i * step, step), step)] = (
                jnp.exp(dist * dist * factor) * inverse
            ).astype(BF16)
            return inner

        return lax.fori_loop(0, cols // step, some, carry)

    lax.fori_loop(0, deep, build_table, 0)
    flat[used:pad] = jnp.zeros((pad - used, cols), F32)
    pl.semaphore_wait(barrier, len(partners))

    for level in range(levels):
        lev_copy(0, level).start()
    site_copy(group).start()

    near_weights, far_weights = vert_weights(lev, levels)
    row_chunks = list(range(rows // 16))
    outer = [c for c in row_chunks if 16 * c < HALO or 16 * c + 16 > rows - HALO]
    inner_chunks = [c for c in row_chunks if c not in outer]

    def lane_loop(body):
        def step(block, carry):
            body(pl.ds(pl.multiple_of(block * BLOCK, BLOCK), BLOCK))
            return carry

        lax.fori_loop(0, blocks, step, 0)

    def vertical(outs, chunks):
        def body(lanes):
            for chunk in chunks:
                first = 16 * chunk
                part = slice(first, first + 16)
                a = [own[j, part, lanes].astype(F32) for j in range(levels)]
                b = [far[j, part, lanes].astype(F32) for j in range(levels)]
                for i in outs:
                    value = mix(near_weights, far_weights, a, b, i)
                    band[i, part, lanes] = value.astype(BF16)
                    top = min(HALO, first + 16) - first
                    if top > 0:
                        edge_f[0, HALO * i + first : HALO * i + first + top, lanes] = value[0:top]
                    skip = max(0, rows - HALO - first)
                    if skip < 16:
                        start = HALO * i + first + skip - (rows - HALO)
                        edge_f[1, start : start + 16 - skip, lanes] = value[skip:16]

        lane_loop(body)

    def send_edges(phase, h):
        def body(lanes):
            for side in range(2):
                part = slice(h * deep * HALO, (h + 1) * deep * HALO)
                edge[phase, h, side, :, lanes] = edge_f[side, part, lanes].astype(BF16)

        lane_loop(body)
        for side in range(2):
            halo_copy(phase, h, side).start()

    def receive_edges(phase, h):
        for side in range(2):
            halo_copy(phase, h, side).wait_recv()

        def body(lanes):
            top = halo[phase, h, 0, :, lanes].astype(F32)
            bottom = halo[phase, h, 1, :, lanes].astype(F32)
            for i in range(deep):
                part = slice(HALO * i, HALO * i + HALO)
                band[h * deep + i, rows : rows + 2 * HALO, lanes] = jnp.concatenate(
                    [top[part], bottom[part]], axis=0
                ).astype(BF16)

        lane_loop(body)

    def smooth(level, block):
        both = jnp.dot(latk[level], band[level, :, block * BLOCK : (block + 1) * BLOCK], preferred_element_type=F32)
        return (both[0:rows] + both[rows : 2 * rows]).astype(BF16)

    def spread_out(block, value):
        for turn in range(blocks):
            start = ((block - turn) % blocks) * BLOCK
            rolled[turn * rows : (turn + 1) * rows, start : start + BLOCK] = value

    def along_longitude(level):
        return jnp.dot(rolled[...], table[level], preferred_element_type=F32)

    def split_rows(chunk):
        return [pl.ds(pl.multiple_of(g * (cols // GROUPS) + chunk * cell, 8), cell) for g in range(GROUPS)]

    def forward(h):
        def body(i, carry):
            level = h * deep + i
            for block in range(blocks):
                spread_out(block, smooth(level, block))
            out = along_longitude(level)
            here = pl.ds(pl.multiple_of(i * rows, 16), rows)
            for block in range(blocks):
                lanes = slice(block * BLOCK, (block + 1) * BLOCK)
                flat[here, lanes] = out[block * rows : (block + 1) * rows] * pert[level, :, lanes].astype(F32)
            return carry

        lax.fori_loop(0, deep, body, 0)

        def turn(i, carry):
            part = pl.ds(pl.multiple_of(i * 128, 128), 128)
            turned[part, :] = flat[:, part].T
            return carry

        lax.fori_loop(0, cols // 128, turn, 0)

        def fill(chunk, carry):
            terms[h, chunk] = pack(jnp.concatenate([turned[part, :] for part in split_rows(chunk)], axis=0))
            return carry

        lax.fori_loop(0, ring, fill, 0)

    def sum_at(h, node):
        value = terms[h, place(-node)]
        for child in children[node]:
            sum_copy(h, child).wait_recv()
            value = value + sum_rx[h, index[child]].astype(F32)
        return value

    def sum_level(h, which):
        for node in nodes:
            if node != 0 and height[node] == which:
                sum_tx[h, index[node]] = sum_at(h, node).astype(BF16)
                sum_copy(h, node).start()

    def sum_root(h):
        value = sum_at(h, 0)
        total[h] = value
        pair_tx[h] = value.astype(BF16)
        pair_copy(h).start()

    def see(h):
        for kind in range(2):
            both = jnp.concatenate([site[g, h, kind] for g in range(GROUPS)], axis=0)
            seen[h, kind] = pack(both)

    def start_gather(h, node):
        for child in children[node]:
            gather_copy(h, child, node).start()

    def adjoint(h):
        pair_copy(h).wait_recv()
        summed = total[h] + pair_rx[h].astype(F32)
        adj[h, z] = (seen[h, 1] * (summed - seen[h, 0])).astype(BF16)
        start_gather(h, 0)
        total[h] = summed

    def gather_level(h, which):
        for node in nodes:
            if node != 0 and depth[node] == which:
                gather_copy(h, node, node).wait_recv()
                start_gather(h, node)

    def increments(h):
        value = unpack(total[h], chunk_rows)
        turned[0:chunk_rows, :] = value
        mine = turned[pl.ds(pl.multiple_of(group * cell, 8), cell), :]
        for i in range(deep):
            inc[h * deep + i] = mine[:, i * rows : (i + 1) * rows]

    def backward(h):
        def open_up(chunk, carry):
            value = unpack(adj[h, chunk].astype(F32), chunk_rows)
            for g, part in enumerate(split_rows(chunk)):
                turned[part, :] = value[g * cell : (g + 1) * cell]
            return carry

        lax.fori_loop(0, ring, open_up, 0)

        def turn(i, carry):
            part = pl.ds(pl.multiple_of(i * 128, 128), 128)
            flat[:, part] = turned[part, :].T
            return carry

        lax.fori_loop(0, cols // 128, turn, 0)

        def body(i, carry):
            level = h * deep + i
            here = pl.ds(pl.multiple_of(i * rows, 16), rows)
            for block in range(blocks):
                lanes = slice(block * BLOCK, (block + 1) * BLOCK)
                spread_out(block, (flat[here, lanes] * pert[level, :, lanes].astype(F32)).astype(BF16))
            out = along_longitude(level)
            reach = pl.ds(pl.multiple_of(level * HALO, 8), HALO)
            for block in range(blocks):
                lanes = slice(block * BLOCK, (block + 1) * BLOCK)
                value = out[block * rows : (block + 1) * rows]
                band[level, 0:rows, lanes] = value.astype(BF16)
                edge_f[0, reach, lanes] = value[0:HALO]
                edge_f[1, reach, lanes] = value[rows - HALO : rows]
            return carry

        lax.fori_loop(0, deep, body, 0)

    def out_copy(level):
        return pltpu.make_async_copy(back.at[level], back_out.at[level], out_sem.at[level])

    def finish(h):
        for i in range(deep):
            level = h * deep + i
            for block in range(blocks):
                back[level, :, block * BLOCK : (block + 1) * BLOCK] = smooth(level, block)
            lev_copy(1, level).start()
            out_copy(level).start()

    halves = range(PAIRS)
    groups_of = [range(h * deep, (h + 1) * deep) for h in halves]
    for level in range(levels):
        lev_copy(0, level).wait_recv()
    for h in halves:
        vertical(groups_of[h], outer)
        send_edges(0, h)
    vertical(range(levels), inner_chunks)
    lax.fori_loop(deep, levels, build_table, 0)
    for h in halves:
        receive_edges(0, h)
        forward(h)
        sum_level(h, 0)
    site_copy(1 - group).wait_recv()
    for h in halves:
        see(h)
    for which in range(1, height[0]):
        for h in halves:
            sum_level(h, which)
    for h in halves:
        sum_root(h)
    for h in halves:
        adjoint(h)
    for h in halves:
        increments(h)
    for which in range(1, max(depth.values()) + 1):
        for h in halves:
            gather_level(h, which)
    for h in halves:
        backward(h)
        send_edges(1, h)
    for h in halves:
        receive_edges(1, h)
        finish(h)
    for level in range(levels):
        lev_copy(1, level).wait_recv()

    for level in range(levels):
        out_copy(level).wait()
        for phase in range(2):
            lev_copy(phase, level).wait_send()
    for h in halves:
        for phase in range(2):
            for side in range(2):
                halo_copy(phase, h, side).wait_send()
        pair_copy(h).wait_send()
        for node in nodes[1:]:
            sum_copy(h, node).wait_send()
            gather_copy(h, node, parent[node]).wait_send()
    site_copy(group).wait_send()


def last_kernel(alpha, near, far, inc, grad, inc_out):
    levels = alpha.shape[0]
    near_weights, far_weights = vert_weights(lax.axis_index("lev"), levels)

    def step(block, carry):
        lanes = pl.ds(pl.multiple_of(block * BLOCK, BLOCK), BLOCK)
        a = [near[j, :, lanes].astype(F32) for j in range(levels)]
        b = [far[j, :, lanes].astype(F32) for j in range(levels)]
        for i in range(levels):
            grad[i, :, lanes] = alpha[i, :, lanes] + mix(near_weights, far_weights, a, b, i)
        return carry

    lax.fori_loop(0, alpha.shape[2] // BLOCK, step, 0)

    @pl.when(pl.program_id(0) == 0)
    def _():
        inc_out[...] = inc[...]


def solution(mesh):
    ring = mesh.shape["member"] // GROUPS
    lat_count, lev_count = mesh.shape["lat"], mesh.shape["lev"]

    def body(alpha_field, perturbation, obs_value, obs_mask, obs_precision, loc_width):
        _, levels, rows, cols = alpha_field.shape
        cell = obs_value.shape[2]
        deep = levels // PAIRS
        pad = round_up(deep * rows, 128)
        packed = packed_rows(GROUPS * cell)
        edges = len(TREE)
        vmem = pl.BlockSpec(memory_space=pltpu.VMEM)
        smem = pl.BlockSpec(memory_space=pltpu.SMEM)
        hbm = pl.BlockSpec(memory_space=pl.ANY)
        dma = pltpu.SemaphoreType.DMA
        full = (levels, rows, cols)
        alpha = alpha_field[0]
        near, far, increment = pl.pallas_call(
            functools.partial(kernel, ring, lat_count, lev_count),
            out_shape=(
                jax.ShapeDtypeStruct(full, BF16),
                jax.ShapeDtypeStruct(full, BF16),
                jax.ShapeDtypeStruct((levels, cell, rows), F32),
            ),
            in_specs=[vmem, vmem, vmem, vmem, smem, smem],
            out_specs=(hbm, hbm, vmem),
            scratch_shapes=[
                pltpu.VMEM(full, BF16),
                pltpu.VMEM(full, BF16),
                pltpu.VMEM((levels, rows + 2 * HALO, cols), BF16),
                pltpu.VMEM((2, levels * HALO, cols), F32),
                pltpu.VMEM((2, PAIRS, 2, deep * HALO, cols), BF16),
                pltpu.VMEM((2, PAIRS, 2, deep * HALO, cols), BF16),
                pltpu.VMEM((levels, 2 * rows, rows + 2 * HALO), BF16),
                pltpu.VMEM((levels, cols, BLOCK), BF16),
                pltpu.VMEM((cols // BLOCK * rows, cols), BF16),
                pltpu.VMEM((pad, cols), F32),
                pltpu.VMEM((cols, pad), F32),
                pltpu.VMEM((PAIRS, ring, packed, 128), F32),
                pltpu.VMEM((PAIRS, edges, packed, 128), BF16),
                pltpu.VMEM((PAIRS, edges, packed, 128), BF16),
                pltpu.VMEM((PAIRS, packed, 128), BF16),
                pltpu.VMEM((PAIRS, packed, 128), BF16),
                pltpu.VMEM((GROUPS, PAIRS, 2, cell, pad), F32),
                pltpu.VMEM((PAIRS, packed, 128), F32),
                pltpu.VMEM((PAIRS, 2, packed, 128), F32),
                pltpu.VMEM((PAIRS, ring, packed, 128), BF16),
                pltpu.VMEM(full, BF16),
                dma((2, levels)), dma((2, levels)),
                dma((2, PAIRS, 2)), dma((2, PAIRS, 2)),
                dma, dma,
                dma((PAIRS, edges)), dma((PAIRS, edges)),
                dma((PAIRS,)), dma((PAIRS,)),
                dma((PAIRS, edges)), dma((PAIRS, edges)),
                dma((levels,)),
            ],
            compiler_params=pltpu.CompilerParams(
                collective_id=0, has_side_effects=True, vmem_limit_bytes=56 * 1024 * 1024
            ),
            name="envar",
        )(
            alpha,
            perturbation[0],
            obs_value.transpose(0, 2, 1),
            obs_mask.transpose(0, 2, 1),
            obs_precision,
            loc_width,
        )
        part = pl.BlockSpec((levels, 16, cols), lambda i: (0, i, 0))
        whole = pl.BlockSpec((levels, cell, rows), lambda i: (0, 0, 0))
        gradient, increment = pl.pallas_call(
            last_kernel,
            grid=(rows // 16,),
            out_shape=(
                jax.ShapeDtypeStruct(full, F32),
                jax.ShapeDtypeStruct((levels, cell, rows), F32),
            ),
            in_specs=[part, part, part, whole],
            out_specs=(part, whole),
            compiler_params=pltpu.CompilerParams(vmem_limit_bytes=32 * 1024 * 1024),
            name="vertical",
        )(alpha, near, far, increment)
        return gradient[None], increment.transpose(0, 2, 1)

    return jax.shard_map(
        body,
        mesh=mesh,
        in_specs=(
            P("member", "lev", "lat", None),
            P("member", "lev", "lat", None),
            P("lev", "lat", "member"),
            P("lev", "lat", "member"),
            P("lev"),
            P("lev"),
        ),
        out_specs=(P("member", "lev", "lat", None), P("lev", "lat", "member")),
        check_vma=False,
    )
```

time: 913 us -> 90.1 us (0.10)
  waiting for transfers between devices: 720 us -> 0 us
  Pallas kernels: 0 us -> 86 us
  blocking collectives: 66.9 us -> 0 us
  other arithmetic: 64 us -> 0 us
  matrix products: 23.7 us -> 0 us
  between operations: 19.3 us -> 0.67 us
    reduce_scatter x1 -> x0, waiting for transfers between devices: 663 us -> none  [body(): lax.psum_scatter(partial_field, 'member', scatter_dimension=2, tiled=True)]
    pallas_call x0 -> x2, Pallas kernels: none -> 86 us  [the longest x1 82.9 us: body(): pl.pallas_call(functools.partial(kernel, ring, lat_count, lev_count), out...]
    all_gather x1 -> x0, blocking collectives: 66.9 us -> none  [body(): lax.all_gather(adjoint_b, 'member', axis=2, tiled=True).astype(jnp.float32)]
    convert_element_type x5 -> x0, other arithmetic: 61.3 us -> none  [the longest x1 24.3 us: body(): smoothed = lat_apply(padded, kernel, band_rows).astype(jnp.bfloat16)]
    all_gather x2 -> x0, waiting for transfers between devices: 44.8 us -> none  [the longest x1 38.7 us: body(): gathered_back = lax.all_gather(smooth_back, 'lev', axis=0, tiled=True)]
    dot_general x4 -> x0, matrix products: 23.7 us -> none  [the longest x1 8.63 us: body(): jnp.einsum('lrn,lnm->lrm', smoothed, tables, preferred_element_type=jnp.f...]
    ppermute x4 -> x0, waiting for transfers between devices: 12.2 us -> none  [the longest x2 7.83 us: extended(): lax.ppermute(head, axis, [((i + 1) % count, i) for i in range(ends)])]
  transfers between devices with their start and end apart: 7 -> 0, of which waited for: 7 -> 0; matrix products, arithmetic and copies ran while one was open for 2% -> 0% of each run, Pallas kernels for 0% -> 0%
where the time goes in v2:
time: 90.1 us; the launch traced here: 89.9 us
  Pallas kernels  86 us (95%)
  local copies, waits for them, and re-layouts  3.17 us (4%)
    pallas_call x1, Pallas kernels, body(): pl.pallas_call(functools.partial(kernel, ring, lat_count, lev_count), out...  82.9 us
    unnamed x8, local copies, waits for them, and re-layouts  3.17 us
    pallas_call x1, Pallas kernels, body(): pl.pallas_call(last_kernel, grid=(rows // 16,), out_shape=(jax.ShapeDtype...  3.08 us

profile of v2, /device:TPU:1, one launch (start us, length us, event | category | flops | bytes accessed | tf_op | source)
XLA Modules:
  0.0 89.9 jit_solution(16329616950909965783)
XLA Ops:
  0.6 0.0 copy-start
  0.6 82.9 %envar.1 = (bf16[4,80,1280]{2,1,0:T(8,128)(2,1)}, bf16[4,80,1280]{2,1,0:T(8,128)(2,1)}, f32[4,40,80]{2,1,0:T(8,128)}) custom-call(f32[4,80,1280]{2,1,0:T(8,128)} %bitcast.6, bf16[4,80,1280]{2,1,0:T(8,128)(2,1)} %bitcast.8, f32[4,40,80]{2,1,0:T(8,128)} %bitcast.9, s32[4,40,80]{2,1,0:T(8,128)} %bitcast.10, f32[4]{0:T(128)} %prec.1, s32[4]{0:T(128)} %width.1), custom_call_target="tpu_custom_call" | custom-call | tf_op jit(solution)/shard_map/envar/pallas_call | solution.py:524
  83.6 0.0 copy-done
  83.6 0.0 copy-start.1
  83.6 1.1 %copy-done.1 = bf16[4,80,1280]{2,1,0:T(8,128)(2,1)S(1)} copy-done((bf16[4,80,1280]{2,1,0:T(8,128)(2,1)S(1)}, bf16[4,80,1280]{2,1,0:T(8,128)(2,1)}, u32[]{:S(2)}) %copy-start.1) | copy-done | bytes 819224
  84.7 0.0 copy-start.2
  84.7 1.1 %copy-done.2 = bf16[4,80,1280]{2,1,0:T(8,128)(2,1)S(1)} copy-done((bf16[4,80,1280]{2,1,0:T(8,128)(2,1)S(1)}, bf16[4,80,1280]{2,1,0:T(8,128)(2,1)}, u32[]{:S(2)}) %copy-start.2) | copy-done | bytes 819224
  85.9 0.0 copy-start.3
  85.9 0.9 copy-done.3
  86.8 3.1 %vertical.1 = (f32[4,80,1280]{2,1,0:T(8,128)}, f32[4,40,80]{2,1,0:T(8,128)}) custom-call(f32[4,80,1280]{2,1,0:T(8,128)S(1)} %bitcast.7, bf16[4,80,1280]{2,1,0:T(8,128)(2,1)S(1)} %copy-done.1, bf16[4,80,1280]{2,1,0:T(8,128)(2,1)S(1)} %copy-done.2, f32[4,40,80]{2,1,0:T(8,128)S(1)} %copy-done.3), custom_call_target="tpu_custom_call" | custom-call | tf_op jit(solution)/shard_map/vertical/pallas_call | solution.py:577
Async XLA Ops:
  0.6 83.0 %copy-start = (f32[1,4,80,1280]{3,2,1,0:T(8,128)S(1)}, f32[1,4,80,1280]{3,2,1,0:T(8,128)}, u32[]{:S(2)}) copy-start(f32[1,4,80,1280]{3,2,1,0:T(8,128)} %param.6) | copy-start | bytes 4915204
  83.6 1.1 %copy-start.1 = (bf16[4,80,1280]{2,1,0:T(8,128)(2,1)S(1)}, bf16[4,80,1280]{2,1,0:T(8,128)(2,1)}, u32[]{:S(2)}) copy-start(bf16[4,80,1280]{2,1,0:T(8,128)(2,1)} %get-tuple-element.7.near) | copy-start | bytes 2457604
  84.7 1.1 %copy-start.2 = (bf16[4,80,1280]{2,1,0:T(8,128)(2,1)S(1)}, bf16[4,80,1280]{2,1,0:T(8,128)(2,1)}, u32[]{:S(2)}) copy-start(bf16[4,80,1280]{2,1,0:T(8,128)(2,1)} %get-tuple-element.8.far) | copy-start | bytes 2457604
  85.9 0.9 copy-start.3

commit v3 on v2

--- a/solution.py
+++ b/solution.py
@@ -21,8 +21,18 @@
 TREE = SIDE + [(-p, -c) for p, c in SIDE if c < 8]
 
 
-def tree_depth(node):
-    return 0 if node == 0 else 1 + tree_depth(next(p for p, c in TREE if c == node))
+class Tree:
+    def __init__(self, pairs):
+        self.nodes = [0] + [c for _, c in pairs]
+        self.index = {c: i for i, (_, c) in enumerate(pairs)}
+        self.parent = {c: p for p, c in pairs}
+        self.children = {n: [c for p, c in pairs if p == n] for n in self.nodes}
+        self.height = {}
+        for n in sorted(self.nodes, key=lambda n: -self.depth(n)):
+            self.height[n] = 1 + max([self.height[c] for c in self.children[n]], default=-1)
+
+    def depth(self, node):
+        return 0 if node == 0 else 1 + self.depth(self.parent[node])
 
 
 def round_up(value, to):
@@ -94,11 +104,11 @@
 
 def kernel(
     ring, lat_count, lev_count,
-    alpha, pert, obs, mask, prec, width,
+    alpha_in, pert_in, obs_in, mask_in, prec, width,
     back_out, far_out, inc,
-    own, far, band, edge_f, edge, halo, latk, table, rolled, flat, turned,
-    terms, sum_tx, sum_rx, pair_tx, pair_rx, site, total, seen, adj, back,
-    lev_send, lev_recv, halo_send, halo_recv, site_send, site_recv,
+    alpha, pert, obs, mask, own, far, band, edge_f, edge, halo, latk, table, rolled, flat, turned,
+    mixed, sum_tx, sum_rx, pair_tx, pair_rx, site, total, seen, adj, back,
+    load_sem, lev_send, lev_recv, halo_send, halo_recv, site_send, site_recv,
     sum_send, sum_recv, pair_send, pair_recv, gather_send, gather_recv, out_sem,
 ):
     levels, rows, cols = alpha.shape
@@ -108,14 +118,7 @@
     pad = flat.shape[0]
     deep = levels // PAIRS
     used = deep * rows
-    nodes = [0] + [c for _, c in TREE]
-    index = {c: i for i, (_, c) in enumerate(TREE)}
-    parent = {c: p for p, c in TREE}
-    children = {n: [c for p, c in TREE if p == n] for n in nodes}
-    depth = {n: tree_depth(n) for n in nodes}
-    height = {}
-    for n in sorted(nodes, key=lambda n: -depth[n]):
-        height[n] = 1 + max([height[c] for c in children[n]], default=-1)
+    trees = [Tree([(s * p, s * c) for p, c in TREE]) for s in (1, -1)]
 
     member = lax.axis_index("member")
     lat = lax.axis_index("lat")
@@ -153,17 +156,17 @@
         return remote(site.at[whose], site.at[whose], site_send, site_recv, pair)
 
     def sum_copy(h, node):
-        i = index[node]
-        to = at(parent[node] - node)
+        i = trees[h].index[node]
+        to = at(trees[h].parent[node] - node)
         return remote(sum_tx.at[h, i], sum_rx.at[h, i], sum_send.at[h, i], sum_recv.at[h, i], to)
 
     def pair_copy(h):
         return remote(pair_tx.at[h], pair_rx.at[h], pair_send.at[h], pair_recv.at[h], pair)
 
     def gather_copy(h, node, holder):
-        i = index[node]
+        i = trees[h].index[node]
         chunk = place(-holder)
-        to = at(node - parent[node])
+        to = at(node - trees[h].parent[node])
         return remote(adj.at[h, chunk], adj.at[h, chunk], gather_send.at[h, i], gather_recv.at[h, i], to)
 
     barrier = pltpu.get_barrier_semaphore()
@@ -172,11 +175,24 @@
     for partner in partners:
         pl.semaphore_signal(barrier, inc=1, device_id=partner, device_id_type=MESH)
 
+    def load(i, level=None):
+        src, dst = ((pert_in, pert), (obs_in, obs), (mask_in, mask))[i] if level is None else (alpha_in.at[level], alpha.at[level])
+        return pltpu.make_async_copy(src, dst, load_sem.at[i])
+
+    for level in range(levels):
+        load(3 + level, level).start()
+    for i in (1, 2, 0):
+        load(i).start()
+
     def round_level(level, carry):
         own[level] = alpha[level].astype(BF16)
         return carry
 
+    for level in range(levels):
+        load(3 + level, level).wait()
     lax.fori_loop(0, levels, round_level, 0)
+    load(1).wait()
+    load(2).wait()
 
     site[group] = jnp.zeros(site.shape[1:], F32)
     for level in range(levels):
@@ -191,16 +207,21 @@
         norm_sq = jnp.sum(
             jnp.where(lane <= 2 * HALO, jnp.exp(-(step * step) / (scale * scale)), 0.0), axis=1, keepdims=True
         )
-        row = lax.broadcasted_iota(jnp.int32, (rows, 128), 0)
-        col = lax.broadcasted_iota(jnp.int32, (rows, 128), 1)
-        is_top = jnp.logical_and(col >= rows, col < rows + HALO)
-        is_bottom = col >= rows + HALO
-        spot = jnp.where(is_top, col - rows - HALO, col)
-        spot = jnp.where(is_bottom, col - HALO, spot)
+        scale = scale[:, 0:1]
+        row = lax.broadcasted_iota(jnp.int32, (rows, BLOCK), 0)
+        col = lax.broadcasted_iota(jnp.int32, (rows, BLOCK), 1)
+        top = rows + HALO * lax.rem(level, deep)
+        bottom = top + HALO * deep
+        is_top = jnp.logical_and(col >= top, col < top + HALO)
+        is_bottom = jnp.logical_and(col >= bottom, col < bottom + HALO)
+        spot = jnp.where(is_top, col - top - HALO, col)
+        spot = jnp.where(is_bottom, col - bottom + rows, spot)
         diff = spot - row
-        keep = jnp.abs(diff) <= HALO
-        keep = jnp.logical_and(keep, jnp.logical_or(jnp.logical_not(is_top), lat > 0))
-        keep = jnp.logical_and(keep, jnp.logical_or(jnp.logical_not(is_bottom), lat < lat_count - 1))
+        keep = jnp.logical_or(
+            col < rows,
+            jnp.logical_or(jnp.logical_and(is_top, lat > 0), jnp.logical_and(is_bottom, lat < lat_count - 1)),
+        )
+        keep = jnp.logical_and(keep, jnp.abs(diff) <= HALO)
         dist = diff.astype(F32)
         weight = jnp.exp(-(dist * dist) / (2.0 * scale * scale)) / jnp.sqrt(norm_sq)
         weight = jnp.where(keep, weight, 0.0)
@@ -233,7 +254,6 @@
 
         return lax.fori_loop(0, cols // step, some, carry)
 
-    lax.fori_loop(0, deep, build_table, 0)
     flat[used:pad] = jnp.zeros((pad - used, cols), F32)
     pl.semaphore_wait(barrier, len(partners))
 
@@ -287,19 +307,14 @@
         for side in range(2):
             halo_copy(phase, h, side).wait_recv()
 
-        def body(lanes):
-            top = halo[phase, h, 0, :, lanes].astype(F32)
-            bottom = halo[phase, h, 1, :, lanes].astype(F32)
-            for i in range(deep):
-                part = slice(HALO * i, HALO * i + HALO)
-                band[h * deep + i, rows : rows + 2 * HALO, lanes] = jnp.concatenate(
-                    [top[part], bottom[part]], axis=0
-                ).astype(BF16)
-
-        lane_loop(body)
-
-    def smooth(level, block):
-        both = jnp.dot(latk[level], band[level, :, block * BLOCK : (block + 1) * BLOCK], preferred_element_type=F32)
+    def smooth(phase, h, level, block):
+        lanes = slice(block * BLOCK, (block + 1) * BLOCK)
+        spare = BLOCK - rows - 2 * deep * HALO
+        field = jnp.concatenate(
+            [band[level, :, lanes], halo[phase, h, 0, :, lanes], halo[phase, h, 1, :, lanes], jnp.zeros((spare, BLOCK), BF16)],
+            axis=0,
+        )
+        both = jnp.dot(latk[level], field, preferred_element_type=F32)
         return (both[0:rows] + both[rows : 2 * rows]).astype(BF16)
 
     def spread_out(block, value):
@@ -317,7 +332,7 @@
         def body(i, carry):
             level = h * deep + i
             for block in range(blocks):
-                spread_out(block, smooth(level, block))
+                spread_out(block, smooth(0, h, level, block))
             out = along_longitude(level)
             here = pl.ds(pl.multiple_of(i * rows, 16), rows)
             for block in range(blocks):
@@ -329,28 +344,22 @@
 
         def turn(i, carry):
             part = pl.ds(pl.multiple_of(i * 128, 128), 128)
-            turned[part, :] = flat[:, part].T
+            turned[h, part, :] = flat[:, part].T
             return carry
 
         lax.fori_loop(0, cols // 128, turn, 0)
 
-        def fill(chunk, carry):
-            terms[h, chunk] = pack(jnp.concatenate([turned[part, :] for part in split_rows(chunk)], axis=0))
-            return carry
-
-        lax.fori_loop(0, ring, fill, 0)
-
     def sum_at(h, node):
-        value = terms[h, place(-node)]
-        for child in children[node]:
+        value = pack(jnp.concatenate([turned[h, part, :] for part in split_rows(place(-node))], axis=0))
+        for child in trees[h].children[node]:
             sum_copy(h, child).wait_recv()
-            value = value + sum_rx[h, index[child]].astype(F32)
+            value = value + sum_rx[h, trees[h].index[child]].astype(F32)
         return value
 
     def sum_level(h, which):
-        for node in nodes:
-            if node != 0 and height[node] == which:
-                sum_tx[h, index[node]] = sum_at(h, node).astype(BF16)
+        for node in trees[h].nodes[1:]:
+            if trees[h].height[node] == which:
+                sum_tx[h, trees[h].index[node]] = sum_at(h, node).astype(BF16)
                 sum_copy(h, node).start()
 
     def sum_root(h):
@@ -365,7 +374,7 @@
             seen[h, kind] = pack(both)
 
     def start_gather(h, node):
-        for child in children[node]:
+        for child in trees[h].children[node]:
             gather_copy(h, child, node).start()
 
     def adjoint(h):
@@ -374,32 +383,35 @@
         adj[h, z] = (seen[h, 1] * (summed - seen[h, 0])).astype(BF16)
         start_gather(h, 0)
         total[h] = summed
+        open_up(h, z)
+
+    def open_up(h, chunk):
+        value = unpack(adj[h, chunk].astype(F32), chunk_rows)
+        for g, part in enumerate(split_rows(chunk)):
+            turned[h, part, :] = value[g * cell : (g + 1) * cell]
 
     def gather_level(h, which):
-        for node in nodes:
-            if node != 0 and depth[node] == which:
-                gather_copy(h, node, node).wait_recv()
-                start_gather(h, node)
+        here = [n for n in trees[h].nodes if trees[h].depth(n) == which]
+        for node in here:
+            gather_copy(h, node, node).wait_recv()
+            start_gather(h, node)
+            if not trees[h].children[node]:
+                open_up(h, place(-node))
+        for node in here:
+            if trees[h].children[node]:
+                open_up(h, place(-node))
 
     def increments(h):
         value = unpack(total[h], chunk_rows)
-        turned[0:chunk_rows, :] = value
-        mine = turned[pl.ds(pl.multiple_of(group * cell, 8), cell), :]
+        mixed[...] = value
+        mine = mixed[pl.ds(pl.multiple_of(group * cell, 8), cell), :]
         for i in range(deep):
             inc[h * deep + i] = mine[:, i * rows : (i + 1) * rows]
 
     def backward(h):
-        def open_up(chunk, carry):
-            value = unpack(adj[h, chunk].astype(F32), chunk_rows)
-            for g, part in enumerate(split_rows(chunk)):
-                turned[part, :] = value[g * cell : (g + 1) * cell]
-            return carry
-
-        lax.fori_loop(0, ring, open_up, 0)
-
         def turn(i, carry):
             part = pl.ds(pl.multiple_of(i * 128, 128), 128)
-            flat[:, part] = turned[part, :].T
+            flat[:, part] = turned[h, part, :].T
             return carry
 
         lax.fori_loop(0, cols // 128, turn, 0)
@@ -415,7 +427,7 @@
             for block in range(blocks):
                 lanes = slice(block * BLOCK, (block + 1) * BLOCK)
                 value = out[block * rows : (block + 1) * rows]
-                band[level, 0:rows, lanes] = value.astype(BF16)
+                band[level, :, lanes] = value.astype(BF16)
                 edge_f[0, reach, lanes] = value[0:HALO]
                 edge_f[1, reach, lanes] = value[rows - HALO : rows]
             return carry
@@ -429,7 +441,7 @@
         for i in range(deep):
             level = h * deep + i
             for block in range(blocks):
-                back[level, :, block * BLOCK : (block + 1) * BLOCK] = smooth(level, block)
+                back[level, :, block * BLOCK : (block + 1) * BLOCK] = smooth(1, h, level, block)
             lev_copy(1, level).start()
             out_copy(level).start()
 
@@ -441,7 +453,8 @@
         vertical(groups_of[h], outer)
         send_edges(0, h)
     vertical(range(levels), inner_chunks)
-    lax.fori_loop(deep, levels, build_table, 0)
+    lax.fori_loop(0, levels, build_table, 0)
+    load(0).wait()
     for h in halves:
         receive_edges(0, h)
         forward(h)
@@ -449,7 +462,7 @@
     site_copy(1 - group).wait_recv()
     for h in halves:
         see(h)
-    for which in range(1, height[0]):
+    for which in range(1, trees[0].height[0]):
         for h in halves:
             sum_level(h, which)
     for h in halves:
@@ -458,7 +471,7 @@
         adjoint(h)
     for h in halves:
         increments(h)
-    for which in range(1, max(depth.values()) + 1):
+    for which in range(1, trees[0].height[0] + 1):
         for h in halves:
             gather_level(h, which)
     for h in halves:
@@ -479,9 +492,9 @@
             for side in range(2):
                 halo_copy(phase, h, side).wait_send()
         pair_copy(h).wait_send()
-        for node in nodes[1:]:
+        for node in trees[h].nodes[1:]:
             sum_copy(h, node).wait_send()
-            gather_copy(h, node, parent[node]).wait_send()
+            gather_copy(h, node, trees[h].parent[node]).wait_send()
     site_copy(group).wait_send()
 
 
@@ -528,21 +541,25 @@
                 jax.ShapeDtypeStruct(full, BF16),
                 jax.ShapeDtypeStruct((levels, cell, rows), F32),
             ),
-            in_specs=[vmem, vmem, vmem, vmem, smem, smem],
+            in_specs=[hbm, hbm, hbm, hbm, smem, smem],
             out_specs=(hbm, hbm, vmem),
             scratch_shapes=[
+                pltpu.VMEM(full, F32),
+                pltpu.VMEM(full, BF16),
+                pltpu.VMEM((levels, cell, rows), F32),
+                pltpu.VMEM((levels, cell, rows), jnp.int32),
                 pltpu.VMEM(full, BF16),
                 pltpu.VMEM(full, BF16),
-                pltpu.VMEM((levels, rows + 2 * HALO, cols), BF16),
+                pltpu.VMEM(full, BF16),
                 pltpu.VMEM((2, levels * HALO, cols), F32),
                 pltpu.VMEM((2, PAIRS, 2, deep * HALO, cols), BF16),
                 pltpu.VMEM((2, PAIRS, 2, deep * HALO, cols), BF16),
-                pltpu.VMEM((levels, 2 * rows, rows + 2 * HALO), BF16),
+                pltpu.VMEM((levels, 2 * rows, BLOCK), BF16),
                 pltpu.VMEM((levels, cols, BLOCK), BF16),
                 pltpu.VMEM((cols // BLOCK * rows, cols), BF16),
                 pltpu.VMEM((pad, cols), F32),
-                pltpu.VMEM((cols, pad), F32),
-                pltpu.VMEM((PAIRS, ring, packed, 128), F32),
+                pltpu.VMEM((PAIRS, cols, pad), F32),
+                pltpu.VMEM((GROUPS * cell, pad), F32),
                 pltpu.VMEM((PAIRS, edges, packed, 128), BF16),
                 pltpu.VMEM((PAIRS, edges, packed, 128), BF16),
                 pltpu.VMEM((PAIRS, packed, 128), BF16),
@@ -552,6 +569,7 @@
                 pltpu.VMEM((PAIRS, 2, packed, 128), F32),
                 pltpu.VMEM((PAIRS, ring, packed, 128), BF16),
                 pltpu.VMEM(full, BF16),
+                dma((3 + levels,)),
                 dma((2, levels)), dma((2, levels)),
                 dma((2, PAIRS, 2)), dma((2, PAIRS, 2)),
                 dma, dma,
@@ -583,7 +601,7 @@
             ),
             in_specs=[part, part, part, whole],
             out_specs=(part, whole),
-            compiler_params=pltpu.CompilerParams(vmem_limit_bytes=32 * 1024 * 1024),
+            compiler_params=pltpu.CompilerParams(vmem_limit_bytes=60 * 1024 * 1024),
             name="vertical",
         )(alpha, near, far, increment)
         return gradient[None], increment.transpose(0, 2, 1)

time: 90.1 us -> 83.5 us (0.927)
  Pallas kernels: 86 us -> 82.6 us
  local copies, waits for them, and re-layouts: 3.17 us -> 0 us
    pallas_call x1, Pallas kernels: 82.9 us -> 77.4 us  [body(): pl.pallas_call(functools.partial(kernel, ring, lat_count, lev_count), out...]
    unnamed x8 -> x0, local copies, waits for them, and re-layouts: 3.17 us -> none
    pallas_call x1, Pallas kernels: 3.08 us -> 5.21 us  [body(): pl.pallas_call(last_kernel, grid=(rows // 16,), out_shape=(jax.ShapeDtype...]
where the time goes in v3:
time: 83.5 us; the launch traced here: 83.2 us
  Pallas kernels  82.6 us (99%)
    pallas_call x1, Pallas kernels, body(): pl.pallas_call(functools.partial(kernel, ring, lat_count, lev_count), out...  77.4 us
    pallas_call x1, Pallas kernels, body(): pl.pallas_call(last_kernel, grid=(rows // 16,), out_shape=(jax.ShapeDtype...  5.21 us

profile of v3, /device:TPU:1, one launch (start us, length us, event | category | flops | bytes accessed | tf_op | source)
XLA Modules:
  0.0 83.2 jit_solution(229773239329848650)
XLA Ops:
  0.6 77.4 %envar.1 = (bf16[4,80,1280]{2,1,0:T(8,128)(2,1)}, bf16[4,80,1280]{2,1,0:T(8,128)(2,1)}, f32[4,40,80]{2,1,0:T(8,128)}) custom-call(f32[4,80,1280]{2,1,0:T(8,128)} %bitcast.6, bf16[4,80,1280]{2,1,0:T(8,128)(2,1)} %bitcast.8, f32[4,40,80]{2,1,0:T(8,128)} %bitcast.9, s32[4,40,80]{2,1,0:T(8,128)} %bitcast.10, f32[4]{0:T(128)} %prec.1, s32[4]{0:T(128)} %width.1), custom_call_target="tpu_custom_call" | custom-call | tf_op jit(solution)/shard_map/envar/pallas_call | solution.py:537
  78.0 5.2 %vertical.1 = (f32[4,80,1280]{2,1,0:T(8,128)}, f32[4,40,80]{2,1,0:T(8,128)}) custom-call(f32[4,80,1280]{2,1,0:T(8,128)} %bitcast.7, bf16[4,80,1280]{2,1,0:T(8,128)(2,1)} %get-tuple-element.7.near, bf16[4,80,1280]{2,1,0:T(8,128)(2,1)} %get-tuple-element.8.far, f32[4,40,80]{2,1,0:T(8,128)} %get-tuple-element.9.inc), custom_call_target="tpu_custom_call" | custom-call | tf_op jit(solution)/shard_map/vertical/pallas_call | solution.py:595

commit v4 on v3

--- a/solution.py
+++ b/solution.py
@@ -104,12 +104,12 @@
 
 def kernel(
     ring, lat_count, lev_count,
-    alpha_in, pert_in, obs_in, mask_in, prec, width,
-    back_out, far_out, inc,
-    alpha, pert, obs, mask, own, far, band, edge_f, edge, halo, latk, table, rolled, flat, turned,
-    mixed, sum_tx, sum_rx, pair_tx, pair_rx, site, total, seen, adj, back,
+    alpha_in, pert_in, obs_in, mask_in, prec_in, width_in,
+    back, far_out, inc,
+    alpha, pert, obs, mask, prec, width, own, far, band, edge_f, edge, halo, latk, table, rolled, flat, turned,
+    mixed, sum_tx, sum_rx, pair_tx, pair_rx, site, total, seen, adj,
     load_sem, lev_send, lev_recv, halo_send, halo_recv, site_send, site_recv,
-    sum_send, sum_recv, pair_send, pair_recv, gather_send, gather_recv, out_sem,
+    sum_send, sum_recv, pair_send, pair_recv, gather_send, gather_recv,
 ):
     levels, rows, cols = alpha.shape
     blocks = cols // BLOCK
@@ -176,12 +176,15 @@
         pl.semaphore_signal(barrier, inc=1, device_id=partner, device_id_type=MESH)
 
     def load(i, level=None):
-        src, dst = ((pert_in, pert), (obs_in, obs), (mask_in, mask))[i] if level is None else (alpha_in.at[level], alpha.at[level])
+        if level is None:
+            src, dst = ((pert_in, pert), (obs_in, obs), (mask_in, mask), (prec_in, prec), (width_in, width))[i]
+        else:
+            src, dst = alpha_in.at[level], alpha.at[level]
         return pltpu.make_async_copy(src, dst, load_sem.at[i])
 
     for level in range(levels):
-        load(3 + level, level).start()
-    for i in (1, 2, 0):
+        load(5 + level, level).start()
+    for i in (3, 4, 1, 2, 0):
         load(i).start()
 
     def round_level(level, carry):
@@ -189,10 +192,10 @@
         return carry
 
     for level in range(levels):
-        load(3 + level, level).wait()
+        load(5 + level, level).wait()
     lax.fori_loop(0, levels, round_level, 0)
-    load(1).wait()
-    load(2).wait()
+    for i in (3, 4, 1, 2):
+        load(i).wait()
 
     site[group] = jnp.zeros(site.shape[1:], F32)
     for level in range(levels):
@@ -254,7 +257,8 @@
 
         return lax.fori_loop(0, cols // step, some, carry)
 
-    flat[used:pad] = jnp.zeros((pad - used, cols), F32)
+    for h in range(PAIRS):
+        turned[h, :, 128:pad] = jnp.zeros((cols, pad - 128), F32)
     pl.semaphore_wait(barrier, len(partners))
 
     for level in range(levels):
@@ -344,7 +348,8 @@
 
         def turn(i, carry):
             part = pl.ds(pl.multiple_of(i * 128, 128), 128)
-            turned[h, part, :] = flat[:, part].T
+            turned[h, part, 0:128] = flat[0:128, part].T
+            turned[h, part, 128:used] = flat[128:used, part].T
             return carry
 
         lax.fori_loop(0, cols // 128, turn, 0)
@@ -411,7 +416,8 @@
     def backward(h):
         def turn(i, carry):
             part = pl.ds(pl.multiple_of(i * 128, 128), 128)
-            flat[:, part] = turned[h, part, :].T
+            flat[0:128, part] = turned[h, part, 0:128].T
+            flat[128:used, part] = turned[h, part, 128:used].T
             return carry
 
         lax.fori_loop(0, cols // 128, turn, 0)
@@ -434,16 +440,12 @@
 
         lax.fori_loop(0, deep, body, 0)
 
-    def out_copy(level):
-        return pltpu.make_async_copy(back.at[level], back_out.at[level], out_sem.at[level])
-
     def finish(h):
         for i in range(deep):
             level = h * deep + i
             for block in range(blocks):
                 back[level, :, block * BLOCK : (block + 1) * BLOCK] = smooth(1, h, level, block)
             lev_copy(1, level).start()
-            out_copy(level).start()
 
     halves = range(PAIRS)
     groups_of = [range(h * deep, (h + 1) * deep) for h in halves]
@@ -471,10 +473,12 @@
         adjoint(h)
     for h in halves:
         increments(h)
-    for which in range(1, trees[0].height[0] + 1):
+    last = trees[0].height[0]
+    for which in range(1, last):
         for h in halves:
             gather_level(h, which)
     for h in halves:
+        gather_level(h, last)
         backward(h)
         send_edges(1, h)
     for h in halves:
@@ -484,7 +488,6 @@
         lev_copy(1, level).wait_recv()
 
     for level in range(levels):
-        out_copy(level).wait()
         for phase in range(2):
             lev_copy(phase, level).wait_send()
     for h in halves:
@@ -498,23 +501,28 @@
     site_copy(group).wait_send()
 
 
-def last_kernel(alpha, near, far, inc, grad, inc_out):
-    levels = alpha.shape[0]
+def last_kernel(alpha, near, far, inc, grad_out, inc_out, grad, store_sem):
+    levels, rows, cols = alpha.shape
     near_weights, far_weights = vert_weights(lax.axis_index("lev"), levels)
-
-    def step(block, carry):
-        lanes = pl.ds(pl.multiple_of(block * BLOCK, BLOCK), BLOCK)
-        a = [near[j, :, lanes].astype(F32) for j in range(levels)]
-        b = [far[j, :, lanes].astype(F32) for j in range(levels)]
-        for i in range(levels):
-            grad[i, :, lanes] = alpha[i, :, lanes] + mix(near_weights, far_weights, a, b, i)
-        return carry
-
-    lax.fori_loop(0, alpha.shape[2] // BLOCK, step, 0)
-
-    @pl.when(pl.program_id(0) == 0)
-    def _():
-        inc_out[...] = inc[...]
+    parts = [pl.ds(16 * i, 16) for i in range(rows // 16)]
+
+    def store(i):
+        return pltpu.make_async_copy(grad.at[:, parts[i]], grad_out.at[:, parts[i]], store_sem.at[i])
+
+    for i, part in enumerate(parts):
+        def step(block, carry):
+            lanes = pl.ds(pl.multiple_of(block * BLOCK, BLOCK), BLOCK)
+            a = [near[j, part, lanes].astype(F32) for j in range(levels)]
+            b = [far[j, part, lanes].astype(F32) for j in range(levels)]
+            for level in range(levels):
+                grad[level, part, lanes] = alpha[level, part, lanes] + mix(near_weights, far_weights, a, b, level)
+            return carry
+
+        lax.fori_loop(0, cols // BLOCK, step, 0)
+        store(i).start()
+    inc_out[...] = inc[...]
+    for i in range(len(parts)):
+        store(i).wait()
 
 
 def solution(mesh):
@@ -529,25 +537,26 @@
         packed = packed_rows(GROUPS * cell)
         edges = len(TREE)
         vmem = pl.BlockSpec(memory_space=pltpu.VMEM)
-        smem = pl.BlockSpec(memory_space=pltpu.SMEM)
-        hbm = pl.BlockSpec(memory_space=pl.ANY)
+        hbm = pl.BlockSpec(memory_space=pltpu.HBM)
         dma = pltpu.SemaphoreType.DMA
         full = (levels, rows, cols)
         alpha = alpha_field[0]
         near, far, increment = pl.pallas_call(
             functools.partial(kernel, ring, lat_count, lev_count),
             out_shape=(
-                jax.ShapeDtypeStruct(full, BF16),
-                jax.ShapeDtypeStruct(full, BF16),
+                pltpu.VMEM(full, BF16),
+                pltpu.VMEM(full, BF16),
                 jax.ShapeDtypeStruct((levels, cell, rows), F32),
             ),
-            in_specs=[hbm, hbm, hbm, hbm, smem, smem],
-            out_specs=(hbm, hbm, vmem),
+            in_specs=[hbm] * 6,
+            out_specs=(vmem, vmem, vmem),
             scratch_shapes=[
                 pltpu.VMEM(full, F32),
                 pltpu.VMEM(full, BF16),
                 pltpu.VMEM((levels, cell, rows), F32),
                 pltpu.VMEM((levels, cell, rows), jnp.int32),
+                pltpu.SMEM((levels,), F32),
+                pltpu.SMEM((levels,), jnp.int32),
                 pltpu.VMEM(full, BF16),
                 pltpu.VMEM(full, BF16),
                 pltpu.VMEM(full, BF16),
@@ -568,40 +577,44 @@
                 pltpu.VMEM((PAIRS, packed, 128), F32),
                 pltpu.VMEM((PAIRS, 2, packed, 128), F32),
                 pltpu.VMEM((PAIRS, ring, packed, 128), BF16),
-                pltpu.VMEM(full, BF16),
-                dma((3 + levels,)),
+                dma((5 + levels,)),
                 dma((2, levels)), dma((2, levels)),
                 dma((2, PAIRS, 2)), dma((2, PAIRS, 2)),
                 dma, dma,
                 dma((PAIRS, edges)), dma((PAIRS, edges)),
                 dma((PAIRS,)), dma((PAIRS,)),
                 dma((PAIRS, edges)), dma((PAIRS, edges)),
-                dma((levels,)),
             ],
             compiler_params=pltpu.CompilerParams(
-                collective_id=0, has_side_effects=True, vmem_limit_bytes=56 * 1024 * 1024
+                collective_id=0, has_side_effects=True, vmem_limit_bytes=32 * 1024 * 1024
             ),
             name="envar",
         )(
-            alpha,
-            perturbation[0],
-            obs_value.transpose(0, 2, 1),
-            obs_mask.transpose(0, 2, 1),
-            obs_precision,
-            loc_width,
+            *[
+                pltpu.with_memory_space_constraint(x, pltpu.HBM)
+                for x in (
+                    alpha,
+                    perturbation[0],
+                    obs_value.transpose(0, 2, 1),
+                    obs_mask.transpose(0, 2, 1),
+                    obs_precision,
+                    loc_width,
+                )
+            ]
         )
-        part = pl.BlockSpec((levels, 16, cols), lambda i: (0, i, 0))
-        whole = pl.BlockSpec((levels, cell, rows), lambda i: (0, 0, 0))
         gradient, increment = pl.pallas_call(
             last_kernel,
-            grid=(rows // 16,),
             out_shape=(
                 jax.ShapeDtypeStruct(full, F32),
                 jax.ShapeDtypeStruct((levels, cell, rows), F32),
             ),
-            in_specs=[part, part, part, whole],
-            out_specs=(part, whole),
-            compiler_params=pltpu.CompilerParams(vmem_limit_bytes=60 * 1024 * 1024),
+            in_specs=[vmem, vmem, vmem, vmem],
+            out_specs=(hbm, vmem),
+            scratch_shapes=[
+                pltpu.VMEM(full, F32),
+                dma((rows // 16,)),
+            ],
+            compiler_params=pltpu.CompilerParams(vmem_limit_bytes=16 * 1024 * 1024),
             name="vertical",
         )(alpha, near, far, increment)
         return gradient[None], increment.transpose(0, 2, 1)

time: 83.5 us -> 78.9 us (0.945)
  Pallas kernels: 82.6 us -> 78.1 us
    pallas_call x1, Pallas kernels: 5.21 us -> 2.56 us  [body(): pl.pallas_call(last_kernel, out_shape=(jax.ShapeDtypeStruct(full, F32), j...]
    pallas_call x1, Pallas kernels: 77.4 us -> 75.6 us  [body(): pl.pallas_call(functools.partial(kernel, ring, lat_count, lev_count), out...]
where the time goes in v4:
time: 78.9 us; the launch traced here: 78.8 us
  Pallas kernels  78.1 us (99%)
    pallas_call x1, Pallas kernels, body(): pl.pallas_call(functools.partial(kernel, ring, lat_count, lev_count), out...  75.6 us
    pallas_call x1, Pallas kernels, body(): pl.pallas_call(last_kernel, out_shape=(jax.ShapeDtypeStruct(full, F32), j...  2.56 us

profile of v4, /device:TPU:1, one launch (start us, length us, event | category | flops | bytes accessed | tf_op | source)
XLA Modules:
  0.0 78.8 jit_solution(5860932820198201516)
XLA Ops:
  0.6 0.0 copy-start
  0.6 75.6 %envar.1 = (bf16[4,80,1280]{2,1,0:T(8,128)(2,1)S(1)}, bf16[4,80,1280]{2,1,0:T(8,128)(2,1)S(1)}, f32[4,40,80]{2,1,0:T(8,128)S(1)}) custom-call(f32[4,80,1280]{2,1,0:T(8,128)} %bitcast.6, bf16[4,80,1280]{2,1,0:T(8,128)(2,1)} %bitcast.8, f32[4,40,80]{2,1,0:T(8,128)} %bitcast.9, s32[4,40,80]{2,1,0:T(8,128)} %bitcast.10, f32[4]{0:T(128)} %prec_in.1, s32[4]{0:T(128)} %width_in.1), custom_call_target="tpu_custom_call" | custom-call | tf_op jit(solution)/shard_map/envar/pallas_call | solution.py:544
  76.2 0.0 copy-done
  76.2 2.6 %vertical.1 = (f32[4,80,1280]{2,1,0:T(8,128)}, f32[4,40,80]{2,1,0:T(8,128)}) custom-call(f32[4,80,1280]{2,1,0:T(8,128)S(1)} %bitcast.7, bf16[4,80,1280]{2,1,0:T(8,128)(2,1)S(1)} %get-tuple-element.7.near, bf16[4,80,1280]{2,1,0:T(8,128)(2,1)S(1)} %get-tuple-element.8.far, f32[4,40,80]{2,1,0:T(8,128)S(1)} %get-tuple-element.9.inc), custom_call_target="tpu_custom_call" | custom-call | tf_op jit(solution)/shard_map/vertical/pallas_call | solution.py:605
Async XLA Ops:
  0.6 75.6 %copy-start = (f32[1,4,80,1280]{3,2,1,0:T(8,128)S(1)}, f32[1,4,80,1280]{3,2,1,0:T(8,128)}, u32[]{:S(2)}) copy-start(f32[1,4,80,1280]{3,2,1,0:T(8,128)} %param.6) | copy-start | bytes 4915204

commit v5 on v4

--- a/solution.py
+++ b/solution.py
@@ -17,8 +17,15 @@
 BF16 = jnp.bfloat16
 MESH = pl.DeviceIdType.MESH
 
-SIDE = [(0, 3), (3, 6), (3, 4), (3, 2), (6, 8), (6, 7), (4, 5), (2, 1)]
-TREE = SIDE + [(-p, -c) for p, c in SIDE if c < 8]
+FIRST = [(0, 3), (0, 1), (3, 6), (3, 4), (1, 2), (6, 8), (6, 7), (4, 5)]
+SECOND = [(0, 3), (3, 6), (3, 4), (3, 2), (6, 8), (6, 7), (4, 5), (2, 1)]
+
+
+def both_sides(side, sign):
+    return [(sign * p, sign * c) for p, c in side] + [(-sign * p, -sign * c) for p, c in side if c < 8]
+
+
+TREES = [both_sides(FIRST, 1), both_sides(SECOND, -1)]
 
 
 class Tree:
@@ -69,7 +76,7 @@
 
 
 def packed_rows(chunk):
-    return round_up(chunk + remainder_rows(chunk), 16)
+    return chunk + remainder_rows(chunk)
 
 
 def pack(value):
@@ -118,7 +125,7 @@
     pad = flat.shape[0]
     deep = levels // PAIRS
     used = deep * rows
-    trees = [Tree([(s * p, s * c) for p, c in TREE]) for s in (1, -1)]
+    trees = [Tree(pairs) for pairs in TREES]
 
     member = lax.axis_index("member")
     lat = lax.axis_index("lat")
@@ -170,7 +177,7 @@
         return remote(adj.at[h, chunk], adj.at[h, chunk], gather_send.at[h, i], gather_recv.at[h, i], to)
 
     barrier = pltpu.get_barrier_semaphore()
-    jumps = sorted({p - c for p, c in TREE} | {c - p for p, c in TREE})
+    jumps = sorted({s * (p - c) for pairs in TREES for p, c in pairs for s in (1, -1)})
     partners = [sibling, south, north, pair] + [at(jump) for jump in jumps]
     for partner in partners:
         pl.semaphore_signal(barrier, inc=1, device_id=partner, device_id_type=MESH)
@@ -194,6 +201,11 @@
     for level in range(levels):
         load(5 + level, level).wait()
     lax.fori_loop(0, levels, round_level, 0)
+    pl.semaphore_wait(barrier, len(partners))
+
+    for level in range(levels):
+        lev_copy(0, level).start()
+
     for i in (3, 4, 1, 2):
         load(i).wait()
 
@@ -202,6 +214,8 @@
         lanes = slice((level % deep) * rows, (level % deep + 1) * rows)
         site[group, level // deep, 0, :, lanes] = obs[level]
         site[group, level // deep, 1, :, lanes] = mask[level].astype(F32) * prec[level]
+
+    site_copy(group).start()
 
     def build_latk(level, carry):
         scale = jnp.full((1, 128), width[level].astype(F32), F32) / 3.0
@@ -259,11 +273,6 @@
 
     for h in range(PAIRS):
         turned[h, :, 128:pad] = jnp.zeros((cols, pad - 128), F32)
-    pl.semaphore_wait(barrier, len(partners))
-
-    for level in range(levels):
-        lev_copy(0, level).start()
-    site_copy(group).start()
 
     near_weights, far_weights = vert_weights(lev, levels)
     row_chunks = list(range(rows // 16))
@@ -464,7 +473,7 @@
     site_copy(1 - group).wait_recv()
     for h in halves:
         see(h)
-    for which in range(1, trees[0].height[0]):
+    for which in range(1, max(tree.height[0] for tree in trees)):
         for h in halves:
             sum_level(h, which)
     for h in halves:
@@ -473,12 +482,13 @@
         adjoint(h)
     for h in halves:
         increments(h)
-    last = trees[0].height[0]
-    for which in range(1, last):
+    lasts = [tree.height[0] for tree in trees]
+    for which in range(1, max(lasts)):
         for h in halves:
-            gather_level(h, which)
-    for h in halves:
-        gather_level(h, last)
+            if which < lasts[h]:
+                gather_level(h, which)
+    for h in halves:
+        gather_level(h, lasts[h])
         backward(h)
         send_edges(1, h)
     for h in halves:
@@ -535,7 +545,7 @@
         deep = levels // PAIRS
         pad = round_up(deep * rows, 128)
         packed = packed_rows(GROUPS * cell)
-        edges = len(TREE)
+        edges = len(TREES[0])
         vmem = pl.BlockSpec(memory_space=pltpu.VMEM)
         hbm = pl.BlockSpec(memory_space=pltpu.HBM)
         dma = pltpu.SemaphoreType.DMA

time: 78.9 us -> 76.9 us (0.975)
  Pallas kernels: 78.1 us -> 76.1 us
    pallas_call x1, Pallas kernels: 75.6 us -> 73.5 us  [body(): pl.pallas_call(functools.partial(kernel, ring, lat_count, lev_count), out...]
where the time goes in v5:
time: 76.9 us; the launch traced here: 76.8 us
  Pallas kernels  76.1 us (99%)
    pallas_call x1, Pallas kernels, body(): pl.pallas_call(functools.partial(kernel, ring, lat_count, lev_count), out...  73.5 us
    pallas_call x1, Pallas kernels, body(): pl.pallas_call(last_kernel, out_shape=(jax.ShapeDtypeStruct(full, F32), j...  2.56 us

profile of v5, /device:TPU:1, one launch (start us, length us, event | category | flops | bytes accessed | tf_op | source)
XLA Modules:
  0.0 76.8 jit_solution(1641775568618101692)
XLA Ops:
  0.6 0.0 copy-start
  0.6 73.5 %envar.1 = (bf16[4,80,1280]{2,1,0:T(8,128)(2,1)S(1)}, bf16[4,80,1280]{2,1,0:T(8,128)(2,1)S(1)}, f32[4,40,80]{2,1,0:T(8,128)S(1)}) custom-call(f32[4,80,1280]{2,1,0:T(8,128)} %bitcast.6, bf16[4,80,1280]{2,1,0:T(8,128)(2,1)} %bitcast.8, f32[4,40,80]{2,1,0:T(8,128)} %bitcast.9, s32[4,40,80]{2,1,0:T(8,128)} %bitcast.10, f32[4]{0:T(128)} %prec_in.1, s32[4]{0:T(128)} %width_in.1), custom_call_target="tpu_custom_call" | custom-call | tf_op jit(solution)/shard_map/envar/pallas_call | solution.py:554
  74.2 0.0 copy-done
  74.2 2.6 %vertical.1 = (f32[4,80,1280]{2,1,0:T(8,128)}, f32[4,40,80]{2,1,0:T(8,128)}) custom-call(f32[4,80,1280]{2,1,0:T(8,128)S(1)} %bitcast.7, bf16[4,80,1280]{2,1,0:T(8,128)(2,1)S(1)} %get-tuple-element.7.near, bf16[4,80,1280]{2,1,0:T(8,128)(2,1)S(1)} %get-tuple-element.8.far, f32[4,40,80]{2,1,0:T(8,128)S(1)} %get-tuple-element.9.inc), custom_call_target="tpu_custom_call" | custom-call | tf_op jit(solution)/shard_map/vertical/pallas_call | solution.py:615
Async XLA Ops:
  0.6 73.6 %copy-start = (f32[1,4,80,1280]{3,2,1,0:T(8,128)S(1)}, f32[1,4,80,1280]{3,2,1,0:T(8,128)}, u32[]{:S(2)}) copy-start(f32[1,4,80,1280]{3,2,1,0:T(8,128)} %param.6) | copy-start | bytes 4915204

commit v6 on v5

--- a/solution.py
+++ b/solution.py
@@ -112,11 +112,11 @@
 def kernel(
     ring, lat_count, lev_count,
     alpha_in, pert_in, obs_in, mask_in, prec_in, width_in,
-    back, far_out, inc,
+    back, far_out, inc_out,
     alpha, pert, obs, mask, prec, width, own, far, band, edge_f, edge, halo, latk, table, rolled, flat, turned,
-    mixed, sum_tx, sum_rx, pair_tx, pair_rx, site, total, seen, adj,
+    mixed, sum_tx, sum_rx, pair_tx, pair_rx, site, total, seen, adj, inc,
     load_sem, lev_send, lev_recv, halo_send, halo_recv, site_send, site_recv,
-    sum_send, sum_recv, pair_send, pair_recv, gather_send, gather_recv,
+    sum_send, sum_recv, pair_send, pair_recv, gather_send, gather_recv, inc_sem,
 ):
     levels, rows, cols = alpha.shape
     blocks = cols // BLOCK
@@ -482,6 +482,8 @@
         adjoint(h)
     for h in halves:
         increments(h)
+    store_inc = pltpu.make_async_copy(inc, inc_out, inc_sem)
+    store_inc.start()
     lasts = [tree.height[0] for tree in trees]
     for which in range(1, max(lasts)):
         for h in halves:
@@ -491,30 +493,37 @@
         gather_level(h, lasts[h])
         backward(h)
         send_edges(1, h)
-    for h in halves:
-        receive_edges(1, h)
-        finish(h)
-    for level in range(levels):
-        lev_copy(1, level).wait_recv()
-
-    for level in range(levels):
-        for phase in range(2):
-            lev_copy(phase, level).wait_send()
-    for h in halves:
-        for phase in range(2):
-            for side in range(2):
-                halo_copy(phase, h, side).wait_send()
+    store_inc.wait()
+    site_copy(group).wait_send()
+    for level in range(levels):
+        lev_copy(0, level).wait_send()
+    for h in halves:
+        for side in range(2):
+            halo_copy(0, h, side).wait_send()
         pair_copy(h).wait_send()
         for node in trees[h].nodes[1:]:
             sum_copy(h, node).wait_send()
             gather_copy(h, node, trees[h].parent[node]).wait_send()
-    site_copy(group).wait_send()
-
-
-def last_kernel(alpha, near, far, inc, grad_out, inc_out, grad, store_sem):
+    for h in halves:
+        receive_edges(1, h)
+        finish(h)
+    for level in range(levels):
+        lev_copy(1, level).wait_recv()
+
+    for level in range(levels):
+        lev_copy(1, level).wait_send()
+    for h in halves:
+        for side in range(2):
+            halo_copy(1, h, side).wait_send()
+
+
+def last_kernel(alpha, near, far, inc, grad_out, inc_out, grad, store_sem, inc_sem):
     levels, rows, cols = alpha.shape
     near_weights, far_weights = vert_weights(lax.axis_index("lev"), levels)
     parts = [pl.ds(16 * i, 16) for i in range(rows // 16)]
+
+    pass_inc = pltpu.make_async_copy(inc, inc_out, inc_sem)
+    pass_inc.start()
 
     def store(i):
         return pltpu.make_async_copy(grad.at[:, parts[i]], grad_out.at[:, parts[i]], store_sem.at[i])
@@ -530,9 +539,9 @@
 
         lax.fori_loop(0, cols // BLOCK, step, 0)
         store(i).start()
-    inc_out[...] = inc[...]
     for i in range(len(parts)):
         store(i).wait()
+    pass_inc.wait()
 
 
 def solution(mesh):
@@ -559,7 +568,7 @@
                 jax.ShapeDtypeStruct((levels, cell, rows), F32),
             ),
             in_specs=[hbm] * 6,
-            out_specs=(vmem, vmem, vmem),
+            out_specs=(vmem, vmem, hbm),
             scratch_shapes=[
                 pltpu.VMEM(full, F32),
                 pltpu.VMEM(full, BF16),
@@ -587,6 +596,7 @@
                 pltpu.VMEM((PAIRS, packed, 128), F32),
                 pltpu.VMEM((PAIRS, 2, packed, 128), F32),
                 pltpu.VMEM((PAIRS, ring, packed, 128), BF16),
+                pltpu.VMEM((levels, cell, rows), F32),
                 dma((5 + levels,)),
                 dma((2, levels)), dma((2, levels)),
                 dma((2, PAIRS, 2)), dma((2, PAIRS, 2)),
@@ -594,6 +604,7 @@
                 dma((PAIRS, edges)), dma((PAIRS, edges)),
                 dma((PAIRS,)), dma((PAIRS,)),
                 dma((PAIRS, edges)), dma((PAIRS, edges)),
+                dma,
             ],
             compiler_params=pltpu.CompilerParams(
                 collective_id=0, has_side_effects=True, vmem_limit_bytes=32 * 1024 * 1024
@@ -618,11 +629,12 @@
                 jax.ShapeDtypeStruct(full, F32),
                 jax.ShapeDtypeStruct((levels, cell, rows), F32),
             ),
-            in_specs=[vmem, vmem, vmem, vmem],
-            out_specs=(hbm, vmem),
+            in_specs=[vmem, vmem, vmem, hbm],
+            out_specs=(hbm, hbm),
             scratch_shapes=[
                 pltpu.VMEM(full, F32),
                 dma((rows // 16,)),
+                dma,
             ],
             compiler_params=pltpu.CompilerParams(vmem_limit_bytes=16 * 1024 * 1024),
             name="vertical",

time: 76.9 us -> 76.2 us (level)
  no operation moved by 1% of the time
where the time goes in v6:
time: 76.2 us; the launch traced here: 76 us
  Pallas kernels  75.4 us (99%)
    pallas_call x1, Pallas kernels, body(): pl.pallas_call(functools.partial(kernel, ring, lat_count, lev_count), out...  73.4 us
    pallas_call x1, Pallas kernels, body(): pl.pallas_call(last_kernel, out_shape=(jax.ShapeDtypeStruct(full, F32), j...  1.94 us

profile of v6, /device:TPU:1, one launch (start us, length us, event | category | flops | bytes accessed | tf_op | source)
XLA Modules:
  0.0 76.0 jit_solution(14063380599963416273)
XLA Ops:
  0.6 0.0 copy-start
  0.6 73.4 %envar.1 = (bf16[4,80,1280]{2,1,0:T(8,128)(2,1)S(1)}, bf16[4,80,1280]{2,1,0:T(8,128)(2,1)S(1)}, f32[4,40,80]{2,1,0:T(8,128)S(1)}) custom-call(f32[4,80,1280]{2,1,0:T(8,128)} %bitcast.6, bf16[4,80,1280]{2,1,0:T(8,128)(2,1)} %bitcast.8, f32[4,40,80]{2,1,0:T(8,128)} %bitcast.9, s32[4,40,80]{2,1,0:T(8,128)} %bitcast.10, f32[4]{0:T(128)} %prec_in.1, s32[4]{0:T(128)} %width_in.1), custom_call_target="tpu_custom_call" | custom-call | tf_op jit(solution)/shard_map/envar/pallas_call | solution.py:563
  74.1 0.0 copy-done
  74.1 1.9 %vertical.1 = (f32[4,80,1280]{2,1,0:T(8,128)}, f32[4,40,80]{2,1,0:T(8,128)}) custom-call(f32[4,80,1280]{2,1,0:T(8,128)S(1)} %bitcast.7, bf16[4,80,1280]{2,1,0:T(8,128)(2,1)S(1)} %get-tuple-element.7.near, bf16[4,80,1280]{2,1,0:T(8,128)(2,1)S(1)} %get-tuple-element.8.far, f32[4,40,80]{2,1,0:T(8,128)S(1)} %get-tuple-element.9.inc), custom_call_target="tpu_custom_call" | custom-call | tf_op jit(solution)/shard_map/vertical/pallas_call | solution.py:626
Async XLA Ops:
  0.6 73.5 %copy-start = (f32[1,4,80,1280]{3,2,1,0:T(8,128)S(1)}, f32[1,4,80,1280]{3,2,1,0:T(8,128)}, u32[]{:S(2)}) copy-start(f32[1,4,80,1280]{3,2,1,0:T(8,128)} %param.6) | copy-start | bytes 4915204

commit v7 on v6

--- a/solution.py
+++ b/solution.py
@@ -458,13 +458,14 @@
 
     halves = range(PAIRS)
     groups_of = [range(h * deep, (h + 1) * deep) for h in halves]
+    lax.fori_loop(0, 1, build_table, 0)
     for level in range(levels):
         lev_copy(0, level).wait_recv()
     for h in halves:
         vertical(groups_of[h], outer)
         send_edges(0, h)
     vertical(range(levels), inner_chunks)
-    lax.fori_loop(0, levels, build_table, 0)
+    lax.fori_loop(1, levels, build_table, 0)
     load(0).wait()
     for h in halves:
         receive_edges(0, h)

time: 76.2 us -> 76.2 us (level)
  no operation moved by 1% of the time
where the time goes in v7:
time: 76.2 us; the launch traced here: 76.1 us
  Pallas kernels  75.4 us (99%)
    pallas_call x1, Pallas kernels, body(): pl.pallas_call(functools.partial(kernel, ring, lat_count, lev_count), out...  73.5 us
    pallas_call x1, Pallas kernels, body(): pl.pallas_call(last_kernel, out_shape=(jax.ShapeDtypeStruct(full, F32), j...  1.94 us

profile of v7, /device:TPU:1, one launch (start us, length us, event | category | flops | bytes accessed | tf_op | source)
XLA Modules:
  0.0 76.1 jit_solution(10173358560107835172)
XLA Ops:
  0.6 0.0 copy-start
  0.6 73.5 %envar.1 = (bf16[4,80,1280]{2,1,0:T(8,128)(2,1)S(1)}, bf16[4,80,1280]{2,1,0:T(8,128)(2,1)S(1)}, f32[4,40,80]{2,1,0:T(8,128)S(1)}) custom-call(f32[4,80,1280]{2,1,0:T(8,128)} %bitcast.6, bf16[4,80,1280]{2,1,0:T(8,128)(2,1)} %bitcast.8, f32[4,40,80]{2,1,0:T(8,128)} %bitcast.9, s32[4,40,80]{2,1,0:T(8,128)} %bitcast.10, f32[4]{0:T(128)} %prec_in.1, s32[4]{0:T(128)} %width_in.1), custom_call_target="tpu_custom_call" | custom-call | tf_op jit(solution)/shard_map/envar/pallas_call | solution.py:564
  74.1 0.0 copy-done
  74.1 1.9 %vertical.1 = (f32[4,80,1280]{2,1,0:T(8,128)}, f32[4,40,80]{2,1,0:T(8,128)}) custom-call(f32[4,80,1280]{2,1,0:T(8,128)S(1)} %bitcast.7, bf16[4,80,1280]{2,1,0:T(8,128)(2,1)S(1)} %get-tuple-element.7.near, bf16[4,80,1280]{2,1,0:T(8,128)(2,1)S(1)} %get-tuple-element.8.far, f32[4,40,80]{2,1,0:T(8,128)S(1)} %get-tuple-element.9.inc), custom_call_target="tpu_custom_call" | custom-call | tf_op jit(solution)/shard_map/vertical/pallas_call | solution.py:627
Async XLA Ops:
  0.6 73.5 %copy-start = (f32[1,4,80,1280]{3,2,1,0:T(8,128)S(1)}, f32[1,4,80,1280]{3,2,1,0:T(8,128)}, u32[]{:S(2)}) copy-start(f32[1,4,80,1280]{3,2,1,0:T(8,128)} %param.6) | copy-start | bytes 4915204
